TPU v7x, 32 devices: a whole 2x2x4 slice. The times are simulated.
32 devices in a mesh: ctx: 8 (over y, x, core), tp: 4 (over z).
Axes of the slice: x: 2, y: 2, z: 4, core: 2. Of those that a mesh axis runs over, the one named last changes fastest.
Arguments:
- inputs: bfloat16 [8192, 4096], P('ctx'), may hold values from -6 to 6
- queries: bfloat16 [8192, 4096], P('ctx', 'tp'), may hold values from -6 to 6
- kv_weight: bfloat16 [4096, 2, 4096], P(None, None, 'tp'), may hold values from -0.09375 to 0.09375
- short_taps: float32 [3, 2, 4096], P(None, None, 'tp'), may hold values from -3 to 3
- filter_taps: bfloat16 [8192, 4096], P('ctx', 'tp'), may hold values from -4 to 4
- skip_gain: float32 [4096], P('tp'), may hold values from 0.5 to 1.5
- out_weight: bfloat16 [4096, 4096], P('tp'), may hold values from -0.09375 to 0.09375
Outputs:
- mixed: bfloat16 [8192, 4096], P(('ctx', 'tp'))
All inputs are finite; a program needn't handle non-finite values.
Results may differ from a plain program's by a relative error of at most 0.015.
Values may be sent and summed in bfloat16 or wider, within the bound.
A program may use at most 320 MiB of HBM per device.

v0:
```python
import math

import jax
import jax.numpy as jnp
from jax import lax
from jax.sharding import PartitionSpec as P


def shifted(value, axis, steps):
    count = lax.axis_size(axis)
    leading, last = (max(0, -steps), min(count, count - steps))
    return lax.ppermute(value, axis, [(source, source + steps) for source in range(leading, last)])


def angle_table(row_index, col_index, period):
    angles = (row_index[:, None] * col_index[None, :] % period).astype(jnp.float32) * (
        2.0 * math.pi / period
    )
    return (jnp.cos(angles), jnp.sin(angles))


def contract(table, data, form):
    return jnp.einsum(form, table, data, precision=lax.Precision.HIGHEST)


def contract_narrow(table, data, form):
    table_high = table.astype(jnp.bfloat16)
    table_low = (table - table_high.astype(jnp.float32)).astype(jnp.bfloat16)
    first = jnp.einsum(form, table_high, data, preferred_element_type=jnp.float32)
    return first + jnp.einsum(form, table_low, data, preferred_element_type=jnp.float32)


def split_factor(length):
    levels = length.bit_length() - 1
    outer = 2 ** ((levels + 1) // 2)
    return (outer, length // outer)


def forward_steps(real_part, imag_part, outer, second, used_rows):
    leading = real_part.shape[:-2]
    channels = real_part.shape[-1]
    real_part = real_part.reshape(leading + (used_rows, second, channels))
    cos_p, sin_p = angle_table(
        jnp.arange(outer, dtype=jnp.int32), jnp.arange(used_rows, dtype=jnp.int32), outer
    )
    form_one = "kp,...pqc->...kqc"
    head_real = contract(cos_p, real_part, form_one)
    head_imag = -contract(sin_p, real_part, form_one)
    imag_part = imag_part.reshape(leading + (used_rows, second, channels))
    head_real = head_real + contract(sin_p, imag_part, form_one)
    head_imag = head_imag + contract(cos_p, imag_part, form_one)
    cos_t, sin_t = angle_table(
        jnp.arange(outer, dtype=jnp.int32), jnp.arange(second, dtype=jnp.int32), outer * second
    )
    cos_t = cos_t[:, :, None]
    sin_t = sin_t[:, :, None]
    turned_real = head_real * cos_t + head_imag * sin_t
    turned_imag = head_imag * cos_t - head_real * sin_t
    cos_q, sin_q = angle_table(
        jnp.arange(second, dtype=jnp.int32), jnp.arange(second, dtype=jnp.int32), second
    )
    form_two = "jq,...kqc->...kjc"
    spec_real = contract(cos_q, turned_real, form_two) + contract(sin_q, turned_imag, form_two)
    spec_imag = contract(cos_q, turned_imag, form_two) - contract(sin_q, turned_real, form_two)
    shape_out = leading + (outer * second, channels)
    return (spec_real.reshape(shape_out), spec_imag.reshape(shape_out))


def inverse_steps(real_part, imag_part, outer, second, kept_rows):
    leading = real_part.shape[:-2]
    channels = real_part.shape[-1]
    real_part = real_part.reshape(leading + (outer, second, channels))
    imag_part = imag_part.reshape(leading + (outer, second, channels))
    cos_q, sin_q = angle_table(
        jnp.arange(second, dtype=jnp.int32), jnp.arange(second, dtype=jnp.int32), second
    )
    form_one = "jq,...kjc->...kqc"
    turned_real = contract(cos_q, real_part, form_one) - contract(sin_q, imag_part, form_one)
    turned_imag = contract(cos_q, imag_part, form_one) + contract(sin_q, real_part, form_one)
    cos_t, sin_t = angle_table(
        jnp.arange(outer, dtype=jnp.int32), jnp.arange(second, dtype=jnp.int32), outer * second
    )
    cos_t = cos_t[:, :, None]
    sin_t = sin_t[:, :, None]
    back_real = turned_real * cos_t - turned_imag * sin_t
    back_imag = turned_imag * cos_t + turned_real * sin_t
    cos_p, sin_p = angle_table(
        jnp.arange(outer, dtype=jnp.int32), jnp.arange(kept_rows, dtype=jnp.int32), outer
    )
    form_two = "kp,...kqc->...pqc"
    shape_out = leading + (kept_rows * second, channels)
    out_real = contract(cos_p, back_real, form_two) - contract(sin_p, back_imag, form_two)
    out_imag = contract(cos_p, back_imag, form_two) + contract(sin_p, back_real, form_two)
    return (out_real.reshape(shape_out), out_imag.reshape(shape_out))


def spread_conv(stacked):
    shards = lax.axis_size("ctx")
    length = stacked.shape[1]
    channels = stacked.shape[2]
    block_rows = length // shards
    padded = 2 * shards * length
    moved = lax.all_to_all(
        stacked.reshape(2, 1, length, channels), "ctx", split_axis=2, concat_axis=1, tiled=True
    )
    cos_c, sin_c = angle_table(
        jnp.arange(2 * shards, dtype=jnp.int32), jnp.arange(shards, dtype=jnp.int32), 2 * shards
    )
    head_real = contract_narrow(cos_c, moved, "kc,gcsd->gksd")
    head_imag = -contract_narrow(sin_c, moved, "kc,gcsd->gksd")
    positions = lax.axis_index("ctx") * block_rows + jnp.arange(block_rows, dtype=jnp.int32)
    cos_t, sin_t = angle_table(jnp.arange(2 * shards, dtype=jnp.int32), positions, padded)
    cos_t = cos_t[:, :, None]
    sin_t = sin_t[:, :, None]
    turned_real = head_real * cos_t + head_imag * sin_t
    turned_imag = head_imag * cos_t - head_real * sin_t
    rows_real, rows_imag = (
        lax.all_to_all(turned_real, "ctx", split_axis=1, concat_axis=2, tiled=True),
        lax.all_to_all(turned_imag, "ctx", split_axis=1, concat_axis=2, tiled=True),
    )
    outer, second = split_factor(length)
    spec_real, spec_imag = forward_steps(rows_real, rows_imag, outer, second, outer)
    prod_real = spec_real[0] * spec_real[1] - spec_imag[0] * spec_imag[1]
    prod_imag = spec_real[0] * spec_imag[1] + spec_imag[0] * spec_real[1]
    local_real, local_imag = inverse_steps(prod_real, prod_imag, outer, second, outer)
    back_real, back_imag = (
        lax.all_to_all(local_real, "ctx", split_axis=1, concat_axis=0, tiled=True),
        lax.all_to_all(local_imag, "ctx", split_axis=1, concat_axis=0, tiled=True),
    )
    undo_real = back_real * cos_t - back_imag * sin_t
    undo_imag = back_imag * cos_t + back_real * sin_t
    blocks = contract(cos_c, undo_real, "kc,ksd->csd") - contract(sin_c, undo_imag, "kc,ksd->csd")
    blocks = blocks / padded
    result = lax.all_to_all(blocks, "ctx", split_axis=0, concat_axis=1, tiled=True)
    return result.reshape(length, channels)


def body(inputs, queries, kv_weight, short_taps, filter_taps, skip_gain, out_weight):
    projected = jnp.einsum(
        "td,dkc->tkc", inputs, kv_weight, preferred_element_type=jnp.float32
    ).astype(jnp.bfloat16)
    carried = shifted(projected[-2:], "ctx", 1)
    extended = jnp.concatenate([carried, projected], 0).astype(jnp.float32)
    smoothed = (
        short_taps[0] * extended[2:]
        + short_taps[1] * extended[1:-1]
        + short_taps[2] * extended[:-2]
    )
    kv_product = (smoothed[:, 0] * smoothed[:, 1]).astype(jnp.bfloat16)
    stacked = jnp.stack([kv_product, filter_taps])
    long_conv = spread_conv(stacked)
    gated = (
        queries.astype(jnp.float32)
        * (long_conv + skip_gain[None, :] * kv_product.astype(jnp.float32))
    ).astype(jnp.bfloat16)
    return lax.psum_scatter(
        jnp.dot(gated, out_weight, preferred_element_type=jnp.float32).astype(jnp.bfloat16),
        "tp",
        scatter_dimension=0,
        tiled=True,
    )


def solution(mesh):
    return jax.shard_map(
        body,
        mesh=mesh,
        in_specs=(
            P("ctx", None),
            P("ctx", "tp"),
            P(None, None, "tp"),
            P(None, None, "tp"),
            P("ctx", "tp"),
            P("tp"),
            P("tp", None),
        ),
        out_specs=P(("ctx", "tp"), None),
        check_vma=False,
    )
```

profile of v0, /device:TPU:0, one launch (start us, length us, event | category | flops | bytes accessed | tf_op | source)
XLA Modules:
  0.0 1395.9 jit_solution(16531752518169056785)
XLA Ops:
  6.5 23.1 %fusion.68 = bf16[1024,2,1024]{2,0,1:T(8,128)(2,1)S(1)} fusion(bf16[4096,2,1024]{2,1,0:T(2,128)(2,1)} %param.9, bf16[1024,4096]{1,0:T(8,128)(2,1)} %param.7), kind=kOutput, calls=%fused_computation.89 | convolution fusion | flops 17181966336 | bytes 29360128 | tf_op jit(solution)/shard_map/td,dkc->tkc/dot_general | solution.py:139
  56.4 48.4 %all-to-all-done = bf16[2,1,1024,1024]{3,0,1,2:T(2,128)(2,1)} async-done(((bf16[2,1,1024,1024]{3,0,1,2:T(2,128)(2,1)}), bf16[2,1,1024,1024]{3,0,1,2:T(2,128)(2,1)}, u32[]{:S(2)}, u32[]{:S(2)}) %all-to-all-start) | async-done | bytes 4194336 | tf_op jit(solution)/shard_map/all_to_all | solution.py:103
  135.0 30.6 %fusion.2 = (f32[2,16,128,1024]{3,1,2,0:T(8,128)}, f32[2,16,128,1024]{3,1,2,0:T(8,128)}) fusion(f32[16,128]{0,1:T(8,128)S(1)} %copy.197, f32[16,128]{0,1:T(8,128)S(1)} %copy.194, f32[2,128,1024,16]{2,3,1,0:T(8,128)} %fusion.66, f32[2,128,1024,16]{2,3,1,0:T(8,128)} %fusion.64, f32[2,128,1024,16]{2,3,1,0:T(8,128)} %fusion.62, ...), kind=kOutput, calls=%fused_computation.8 | convolution fusion | flops 104859904 | bytes 88096768 | tf_op jit(solution)/shard_map/kc,gcsd->gksd/dot_general | solution.py:30
  165.6 17.7 %copy.203 = f32[2,16,128,1024]{3,2,0,1:T(8,128)} copy(f32[2,16,128,1024]{3,1,2,0:T(8,128)} %get-tuple-element.6) | data formatting | bytes 33554432 | tf_op jit(solution)/shard_map/sub | solution.py:116
  189.1 17.8 %copy.198 = f32[2,16,128,1024]{3,2,0,1:T(8,128)} copy(f32[2,16,128,1024]{3,1,2,0:T(8,128)} %get-tuple-element.5) | data formatting | bytes 33554432 | tf_op jit(solution)/shard_map/add | solution.py:115
  206.9 166.1 %all-to-all-done.2 = f32[2,16,128,1024]{3,2,0,1:T(8,128)} async-done(((f32[2,16,128,1024]{3,2,0,1:T(8,128)}), f32[2,16,128,1024]{3,2,0,1:T(8,128)}, u32[]{:S(2)}, u32[]{:S(2)}) %all-to-all-start.2) | async-done | bytes 16777248 | tf_op jit(solution)/shard_map/all_to_all | solution.py:119
  380.3 11.9 copy.205
  392.2 36.5 %fusion.14 = f32[2,2,32,1024,32]{3,4,2,1,0:T(8,128)} fusion(f32[2,2,32,32,1024]{4,3,2,1,0:T(8,128)} %bitcast.184), kind=kOutput, calls=%fused_computation.26 | convolution fusion | flops 1610627072 | bytes 33554432 | tf_op jit(solution)/shard_map/kp,...pqc->...kqc/dot_general | solution.py:23
  428.7 36.9 %fusion.16 = f32[2,2,32,1024,32]{3,4,2,1,0:T(8,128)} fusion(f32[2,2,32,32,1024]{4,3,2,1,0:T(8,128)} %bitcast.185), kind=kOutput, calls=%fused_computation.28 | convolution fusion | flops 1610627072 | bytes 33554432 | tf_op jit(solution)/shard_map/kp,...pqc->...kqc/dot_general | solution.py:23
  465.6 97.2 %all-to-all-done.1 = f32[2,16,128,1024]{3,2,0,1:T(8,128)} async-done(((f32[2,16,128,1024]{3,2,0,1:T(8,128)}), f32[2,16,128,1024]{3,2,0,1:T(8,128)}, u32[]{:S(2)}, u32[]{:S(2)}) %all-to-all-start.1) | async-done | bytes 16777248 | tf_op jit(solution)/shard_map/all_to_all | solution.py:118
  562.8 11.8 copy.200
  574.6 36.3 %fusion.20 = f32[2,2,32,1024,32]{3,4,2,1,0:T(8,128)} fusion(f32[2,2,32,32,1024]{4,3,2,1,0:T(8,128)} %bitcast.186), kind=kOutput, calls=%fused_computation.32 | convolution fusion | flops 1610627072 | bytes 33554432 | tf_op jit(solution)/shard_map/kp,...pqc->...kqc/dot_general | solution.py:23
  610.9 51.6 %fusion = (f32[2,2,32,32,1024]{4,2,3,1,0:T(8,128)}, f32[2,2,32,32,1024]{4,2,3,1,0:T(8,128)}) fusion(f32[32,32]{0,1:T(8,128)S(1)} %get-tuple-element.20, f32[32,32]{0,1:T(8,128)S(1)} %get-tuple-element.21, f32[2,2,32,1024,32]{3,4,2,1,0:T(8,128)} %fusion.20, f32[2,2,32,1024,32]{3,4,2,1,0:T(8,128)} %fusion.16, f32[2,2,32,1024,32]{3,4,2,1,0:T(8,128)} %fusion.14, ...), kind=kOutput, calls=%fused_computation.2 | convolution fusion | flops 1648375808 | bytes 100671488 | tf_op jit(solution)/shard_map/kp,...pqc->...kqc/dot_general | solution.py:23
  662.5 36.8 %fusion.8 = f32[2,2,32,1024,32]{3,4,2,1,0:T(8,128)} fusion(f32[2,2,32,32,1024]{4,2,3,1,0:T(8,128)} %get-tuple-element.8), kind=kOutput, calls=%fused_computation.20 | convolution fusion | flops 1610627072 | bytes 33554432 | tf_op jit(solution)/shard_map/jq,...kqc->...kjc/dot_general | solution.py:23
  699.4 36.5 %fusion.6 = f32[2,2,32,1024,32]{3,4,2,1,0:T(8,128)} fusion(f32[2,2,32,32,1024]{4,2,3,1,0:T(8,128)} %get-tuple-element.8), kind=kOutput, calls=%fused_computation.18 | convolution fusion | flops 1610627072 | bytes 33554432 | tf_op jit(solution)/shard_map/jq,...kqc->...kjc/dot_general | solution.py:23
  735.9 32.5 %add_bitcast_fusion = f32[2,2,32,32,1024]{4,3,2,1,0:T(8,128)} fusion(f32[2,2,32,1024,32]{3,4,2,1,0:T(8,128)} %fusion.8, f32[2,2,32,32,1024]{4,2,3,1,0:T(8,128)} %get-tuple-element.7), kind=kOutput, calls=%fused_computation.15 | convolution fusion | flops 1614821376 | bytes 50331648 | tf_op jit(solution)/shard_map/jq,...kqc->...kjc/dot_general | solution.py:23
  768.5 32.3 %subtract_bitcast_fusion = f32[2,2,32,32,1024]{4,3,2,1,0:T(8,128)} fusion(f32[2,2,32,1024,32]{3,4,2,1,0:T(8,128)} %fusion.6, f32[2,2,32,32,1024]{4,2,3,1,0:T(8,128)} %get-tuple-element.7), kind=kOutput, calls=%fused_computation.14 | convolution fusion | flops 1614821376 | bytes 50331648 | tf_op jit(solution)/shard_map/jq,...kqc->...kjc/dot_general | solution.py:23
  800.7 18.6 %multiply_subtract_fusion = (f32[1,2,32,32,1024]{4,3,2,1,0:T(8,128)}, f32[1,2,32,32,1024]{4,3,2,1,0:T(8,128)}) fusion(f32[2,2,32,32,1024]{4,3,2,1,0:T(8,128)} %subtract_bitcast_fusion, f32[2,2,32,32,1024]{4,3,2,1,0:T(8,128)} %add_bitcast_fusion), kind=kLoop, calls=%fused_computation.63 | loop fusion | flops 12582912 | bytes 50331648 | tf_op jit(solution)/shard_map/sub | solution.py:123
  819.4 13.2 fusion.26
  854.5 25.0 %subtract_bitcast_fusion.2 = (f32[2,32,32,1024]{3,2,1,0:T(8,128)}, f32[2,32,32,1024]{3,2,1,0:T(8,128)}) fusion(f32[32,32]{1,0:T(8,128)S(1)} %copy-done.6, f32[32,32]{1,0:T(8,128)S(1)} %copy-done.5, f32[2,32,1024,32]{2,3,1,0:T(8,128)} %fusion.26, f32[2,32,1024,32]{2,3,1,0:T(8,128)} %fusion.30, f32[2,32,1024,32]{2,3,1,0:T(8,128)} %fusion.28, ...), kind=kOutput, calls=%fused_computation.61 | convolution fusion | flops 822097920 | bytes 50339840 | tf_op jit(solution)/shard_map/jq,...kjc->...kqc/dot_general | solution.py:23
  879.4 20.0 %fusion.41 = f32[2,32,1024,32]{2,3,1,0:T(8,128)S(1)} fusion(f32[2,32,32,1024]{3,2,1,0:T(8,128)} %get-tuple-element.10), kind=kOutput, calls=%fused_computation.66 | convolution fusion | flops 805320704 | bytes 16777216 | tf_op jit(solution)/shard_map/kp,...kqc->...pqc/dot_general | solution.py:23
  899.4 18.4 %subtract_bitcast_fusion.1 = f32[2,32,32,1024]{3,1,2,0:T(8,128)S(1)} fusion(f32[2,32,1024,32]{2,3,1,0:T(8,128)S(1)} %fusion.41, f32[2,32,32,1024]{3,2,1,0:T(8,128)S(1)} %copy-done), kind=kOutput, calls=%fused_computation.59 | convolution fusion | flops 807417856 | bytes 25165824 | tf_op jit(solution)/shard_map/kp,...kqc->...pqc/dot_general | solution.py:23
  922.7 13.0 copy.225
  940.9 19.2 %fusion.39 = f32[2,32,1024,32]{2,3,1,0:T(8,128)S(1)} fusion(f32[2,32,32,1024]{3,2,1,0:T(8,128)} %get-tuple-element.10), kind=kOutput, calls=%fused_computation.64 | convolution fusion | flops 805320704 | bytes 16777216 | tf_op jit(solution)/shard_map/kp,...kqc->...pqc/dot_general | solution.py:23
  960.1 20.9 %add_bitcast_fusion.1 = f32[2,32,32,1024]{3,1,2,0:T(8,128)S(1)} fusion(f32[2,32,1024,32]{2,3,1,0:T(8,128)S(1)} %fusion.39, f32[2,32,32,1024]{3,2,1,0:T(8,128)} %get-tuple-element.9), kind=kOutput, calls=%fused_computation.58 | convolution fusion | flops 807417856 | bytes 25165824 | tf_op jit(solution)/shard_map/kp,...kqc->...pqc/dot_general | solution.py:23
  985.8 12.9 copy.231
  998.8 36.2 %all-to-all-done.3 = f32[2,1024,1024]{2,0,1:T(2,128)} async-done(((f32[2,1024,1024]{2,0,1:T(2,128)}), f32[2,1024,1024]{2,0,1:T(2,128)}, u32[]{:S(2)}, u32[]{:S(2)}) %all-to-all-start.3) | async-done | bytes 8388640 | tf_op jit(solution)/shard_map/all_to_all | solution.py:127
  1050.4 83.6 %all-to-all-done.4 = f32[2,1024,1024]{2,0,1:T(2,128)} async-done(((f32[2,1024,1024]{2,0,1:T(2,128)}), f32[2,1024,1024]{2,0,1:T(2,128)}, u32[]{:S(2)}, u32[]{:S(2)}) %all-to-all-start.4) | async-done | bytes 8388640 | tf_op jit(solution)/shard_map/all_to_all | solution.py:128
  1151.2 13.0 fusion.35
  1176.8 51.8 %all_to_all.87 = f32[8,128,1024]{2,1,0:T(8,128)S(1)} all-to-all(f32[8,128,1024]{2,1,0:T(8,128)S(1)} %copy.236), channel_id=1, replica_groups=mesh['ctx'=8,'tp'=4] {'ctx'}, dimensions={0} | all-to-all | bytes 8388608 | tf_op jit(solution)/shard_map/all_to_all | solution.py:134
  1230.5 14.3 %convolution_convert_fusion = bf16[1024,4096]{1,0:T(8,128)(2,1)} fusion(bf16[1024,1024]{1,0:T(8,128)(2,1)S(1)} %fusion.56, bf16[1024,4096]{1,0:T(8,128)(2,1)} %param.13), kind=kOutput, calls=%fused_computation.72 | convolution fusion | flops 8594128896 | bytes 18874368 | tf_op jit(solution)/shard_map/dot_general | solution.py:157
  1244.8 144.0 %reduce-scatter.2.cloned.1.call-done = bf16[256,4096]{1,0:T(8,128)(2,1)} async-done(((bf16[1024,4096]{1,0:T(8,128)(2,1)}), bf16[256,4096]{1,0:T(8,128)(2,1)}) %reduce-scatter.2.cloned.1.call-update) | async-done | bytes 2097168 | tf_op jit(solution)/shard_map/reduce_scatter | solution.py:156
  (80 shorter events, 153.6 us)
Async XLA Ops:
  6.5 25.5 %copy-start.11 = (f32[3,2,1024]{2,1,0:T(2,128)S(1)}, f32[3,2,1024]{2,1,0:T(2,128)}, u32[]{:S(2)}) copy-start(f32[3,2,1024]{2,1,0:T(2,128)} %param.10) | copy-start | bytes 73732
  29.7 3.2 collective-permute-start
  36.6 3.3 copy-start.1
  39.9 1.6 copy-start.4
  48.2 56.7 %all-to-all-start = ((bf16[2,1,1024,1024]{3,0,1,2:T(2,128)(2,1)}), bf16[2,1,1024,1024]{3,0,1,2:T(2,128)(2,1)}, u32[]{:S(2)}, u32[]{:S(2)}) async-start(bf16[2,1,1024,1024]{3,0,1,2:T(2,128)(2,1)} %copy.190), calls=%async_computation | async-start | bytes 8388608 | tf_op jit(solution)/shard_map/all_to_all | solution.py:103
  55.7 0.6 copy-start.7
  55.8 61.5 %copy-start.9 = (f32[16,128]{1,0:T(8,128)}, f32[16,128]{1,0:T(8,128)S(1)}, u32[]{:S(2)}) copy-start(f32[16,128]{1,0:T(8,128)S(1)} %get-tuple-element.19) | copy-start | bytes 24580
  183.3 189.7 %all-to-all-start.2 = ((f32[2,16,128,1024]{3,2,0,1:T(8,128)}), f32[2,16,128,1024]{3,2,0,1:T(8,128)}, u32[]{:S(2)}, u32[]{:S(2)}) async-start(f32[2,16,128,1024]{3,2,0,1:T(8,128)} %copy.203), calls=%async_computation.2 | async-start | bytes 33554432 | tf_op jit(solution)/shard_map/all_to_all | solution.py:119
  373.1 189.7 %all-to-all-start.1 = ((f32[2,16,128,1024]{3,2,0,1:T(8,128)}), f32[2,16,128,1024]{3,2,0,1:T(8,128)}, u32[]{:S(2)}, u32[]{:S(2)}) async-start(f32[2,16,128,1024]{3,2,0,1:T(8,128)} %copy.198), calls=%async_computation.1 | async-start | bytes 33554432 | tf_op jit(solution)/shard_map/all_to_all | solution.py:118
  819.4 13.2 copy-start.2
  819.4 24.0 %slice-start.2 = ((s8[8388608]{0:T(1024)(128)(4,1)}), s8[4194304]{0:T(1024)(128)(4,1)S(1)}, s32[]{:S(2)}) async-start(s8[8388608]{0:T(1024)(128)(4,1)} %bitcast.194), calls=%async_computation.10 | async-start | bytes 8388608
  832.6 10.8 slice-start.3
  843.4 11.0 copy-start.5
  843.4 11.0 copy-start.6
  879.4 20.0 %copy-start = (f32[2,32,32,1024]{3,2,1,0:T(8,128)S(1)}, f32[2,32,32,1024]{3,2,1,0:T(8,128)}, u32[]{:S(2)}) copy-start(f32[2,32,32,1024]{3,2,1,0:T(8,128)} %get-tuple-element.9) | copy-start | bytes 25165828
  935.7 99.3 %all-to-all-start.3 = ((f32[2,1024,1024]{2,0,1:T(2,128)}), f32[2,1024,1024]{2,0,1:T(2,128)}, u32[]{:S(2)}, u32[]{:S(2)}) async-start(f32[2,1024,1024]{2,0,1:T(2,128)} %copy.225), calls=%async_computation.3 | async-start | bytes 16777216 | tf_op jit(solution)/shard_map/all_to_all | solution.py:127
  1035.0 99.0 %all-to-all-start.4 = ((f32[2,1024,1024]{2,0,1:T(2,128)}), f32[2,1024,1024]{2,0,1:T(2,128)}, u32[]{:S(2)}, u32[]{:S(2)}) async-start(f32[2,1024,1024]{2,0,1:T(2,128)} %copy.231), calls=%async_computation.4 | async-start | bytes 16777216 | tf_op jit(solution)/shard_map/all_to_all | solution.py:128
  1039.9 348.9 %reduce-scatter.2.cloned.1.call-start = ((), (), s32[]{:S(2)}) async-start(), calls=%async_computation.7 | async-start | bytes 10485760 | tf_op jit(solution)/shard_map/reduce_scatter | solution.py:156
  1134.0 10.4 slice-start.4
  1140.2 4.2 slice-start.5
  1140.2 4.2 copy-start.8
  1140.2 4.2 copy-start.10
  1174.2 54.5 %slice-start = ((s8[8388608]{0:T(1024)(128)(4,1)}), s8[4194304]{0:T(1024)(128)(4,1)S(1)}, s32[]{:S(2)}) async-start(s8[8388608]{0:T(1024)(128)(4,1)} %bitcast.192), calls=%async_computation.8 | async-start | bytes 8388608
  1174.2 54.5 %copy-start.3 = (bf16[1024,1024]{1,0:T(8,128)(2,1)S(1)}, bf16[1024,1024]{1,0:T(8,128)(2,1)}, u32[]{:S(2)}) copy-start(bf16[1024,1024]{1,0:T(8,128)(2,1)} %param.8) | copy-start | bytes 6291460
  1174.2 54.5 %copy-start.12 = (f32[1024]{0:T(1024)S(1)}, f32[1024]{0:T(1024)}, u32[]{:S(2)}) copy-start(f32[1024]{0:T(1024)} %param.12) | copy-start | bytes 12292
  1176.8 51.8 %slice-start.1 = ((s8[8388608]{0:T(1024)(128)(4,1)}), s8[4194304]{0:T(1024)(128)(4,1)S(1)}, s32[]{:S(2)}) async-start(s8[8388608]{0:T(1024)(128)(4,1)} %bitcast.192), calls=%async_computation.9 | async-start | bytes 8388608
Sparse Core Ops, SparseCore 0:
  1245.0 143.8 reduce-scatter.1
where the time goes:
time: 1400 us
  waiting for transfers between devices  576 us (41%)
  matrix products  556 us (40%)
  local copies, waits for them, and re-layouts  134 us (10%)
  blocking collectives  51.8 us (4%)
  other arithmetic  32.2 us (2%)
  starting transfers between devices  31.8 us (2%)
  between operations  14 us (1%)
    dot_general x18, matrix products, contract(): return jnp.einsum(form, table, data, precision=lax.Precision.HIGHEST)  461 us
    all_to_all x1, waiting for transfers between devices, spread_conv(): lax.all_to_all(turned_imag, 'ctx', split_axis=1, concat_axis=2, tiled=True)  166 us
    reduce_scatter x1, waiting for transfers between devices, body(): lax.psum_scatter(jnp.dot(gated, out_weight, preferred_element_type=jnp.fl...  144 us
    all_to_all x1, waiting for transfers between devices, spread_conv(): lax.all_to_all(turned_real, 'ctx', split_axis=1, concat_axis=2, tiled=True)  97.2 us
    all_to_all x1, waiting for transfers between devices, spread_conv(): lax.all_to_all(local_imag, 'ctx', split_axis=1, concat_axis=0, tiled=True)  83.6 us
    all_to_all x1, blocking collectives, spread_conv(): lax.all_to_all(blocks, 'ctx', split_axis=0, concat_axis=1, tiled=True)  51.8 us
    all_to_all x1, waiting for transfers between devices, spread_conv(): lax.all_to_all(stacked.reshape(2, 1, length, channels), 'ctx', split_axis...  48.4 us
    dot_general x2, matrix products, contract_narrow(): jnp.einsum(form, table_low, data, preferred_element_type=jnp.float32)  39.5 us
  transfers between devices with their start and end apart: 7, of which 7 were waited for; matrix products, arithmetic and copies ran while one was open for 12% of the time, Pallas kernels for 0%

commit v1 on v0

v1 whole, which is shorter than its diff:
```python
import functools

import jax
import jax.numpy as jnp
import ml_dtypes
import numpy as np
from jax import lax
from jax.experimental import pallas as pl
from jax.experimental.pallas import tpu as pltpu
from jax.sharding import PartitionSpec as P

SECOND = 128
SUB = 8


def shifted(value, axis, steps):
    count = lax.axis_size(axis)
    leading, last = (max(0, -steps), min(count, count - steps))
    return lax.ppermute(value, axis, [(source, source + steps) for source in range(leading, last)])


@functools.lru_cache(maxsize=None)
def tables(length):
    padded = 2 * length
    outer = padded // SECOND
    used = outer // 2
    half = outer // 2 + 1
    k1 = np.arange(half)
    head_angle = 2.0 * np.pi / outer * (k1[:, None] * np.arange(used)[None, :] % outer)
    head = np.stack([np.cos(head_angle), -np.sin(head_angle)], 1).reshape(2 * half, used)
    spread = np.zeros((2 * half, SUB, used, SUB), np.float32)
    for s in range(SUB):
        spread[:, s, :, s] = head
    first = spread.reshape(2 * half * SUB, used * SUB)
    q = np.arange(SECOND)
    freq = k1[:, None] + outer * np.arange(SECOND)[None, :]
    angle = 2.0 * np.pi / padded * (freq[:, :, None] * q[None, None, :] % padded)
    cos_t, sin_t = np.cos(angle).astype(np.float32), -np.sin(angle).astype(np.float32)
    mid = np.concatenate(
        [np.concatenate([cos_t, -sin_t], 2), np.concatenate([sin_t, cos_t], 2)], 1
    )
    narrow = lambda t: np.ascontiguousarray(t).astype(ml_dtypes.bfloat16)
    return narrow(first), narrow(first.T), narrow(mid), narrow(mid.transpose(0, 2, 1))


def conv_kernel(
    half, per_step, scale, kv_ref, taps_ref, first_ref, last_ref, fwd_ref, inv_ref, out_ref, a_ref, b_ref
):
    used = kv_ref.shape[0]
    channels = kv_ref.shape[2]
    step = pl.program_id(0)
    f32 = jnp.float32

    @pl.when(step == 0)
    def _():
        @pl.loop(0, SECOND // 16)
        def _(block):
            rows = pl.ds(pl.multiple_of(block * 16, 16), 16)
            data = jnp.concatenate([kv_ref[:, rows, :], taps_ref[:, rows, :]], axis=2).astype(f32)
            for part in range(2):
                piece = data[:, part * SUB : (part + 1) * SUB, :]
                piece = piece.reshape(used * SUB, 2 * channels).astype(jnp.bfloat16)
                got = jnp.dot(first_ref[...], piece, preferred_element_type=f32)
                into = pl.ds(pl.multiple_of(block * 16 + part * SUB, SUB), SUB)
                a_ref[:, into, :] = got.reshape(2 * half, SUB, 2 * channels)

    for j in range(per_step):
        k1 = step * per_step + j
        pair = pl.ds(2 * k1, 2)
        turned = a_ref[pair].reshape(2 * SECOND, 2 * channels).astype(jnp.bfloat16)
        spec = jnp.dot(fwd_ref[j], turned, preferred_element_type=f32)
        sig_r, sig_i = spec[:SECOND, :channels], spec[SECOND:, :channels]
        tap_r, tap_i = spec[:SECOND, channels:], spec[SECOND:, channels:]
        weight = jnp.where((k1 == 0) | (k1 == half - 1), scale, 2.0 * scale).astype(f32)
        tap_r, tap_i = tap_r * weight, tap_i * weight
        prod_r = sig_r * tap_r - sig_i * tap_i
        prod_i = sig_r * tap_i + sig_i * tap_r
        prod = jnp.concatenate([prod_r, prod_i], 0).astype(jnp.bfloat16)
        back = jnp.dot(inv_ref[j], prod, preferred_element_type=f32)
        b_ref[pair] = back.reshape(2, SECOND, channels)

    @pl.when(step == pl.num_programs(0) - 1)
    def _():
        @pl.loop(0, SECOND // 16)
        def _(block):
            pieces = []
            for part in range(2):
                rows = pl.ds(pl.multiple_of(block * 16 + part * SUB, SUB), SUB)
                piece = b_ref[:, rows, :].reshape(2 * half * SUB, channels).astype(jnp.bfloat16)
                got = jnp.dot(last_ref[...], piece, preferred_element_type=f32)
                pieces.append(got.reshape(used, SUB, channels))
            into = pl.ds(pl.multiple_of(block * 16, 16), 16)
            out_ref[:, into, :] = jnp.concatenate(pieces, axis=1).astype(out_ref.dtype)


def local_conv(kv, taps):
    length, channels = kv.shape
    first, last, fwd, inv = tables(length)
    used = length // SECOND
    half = fwd.shape[0]
    per_step = max(n for n in range(1, 6) if half % n == 0)
    shape = (used, SECOND, channels)
    whole = lambda *dims: pl.BlockSpec(dims, lambda i: (0,) * len(dims), pipeline_mode=pl.Buffered(1))
    table = pl.BlockSpec((per_step, 2 * SECOND, 2 * SECOND), lambda i: (i, 0, 0))
    out = pl.pallas_call(
        functools.partial(conv_kernel, half, per_step, 0.5 / length),
        grid=(half // per_step,),
        out_shape=jax.ShapeDtypeStruct(shape, jnp.bfloat16),
        in_specs=[whole(*shape), whole(*shape), whole(*first.shape), whole(*last.shape), table, table],
        out_specs=whole(*shape),
        scratch_shapes=[
            pltpu.VMEM((2 * half, SECOND, 2 * channels), jnp.float32),
            pltpu.VMEM((2 * half, SECOND, channels), jnp.float32),
        ],
        compiler_params=pltpu.CompilerParams(vmem_limit_bytes=60 * 2**20),
    )(kv.reshape(shape), taps.reshape(shape), first, last, fwd, inv)
    return out.reshape(length, channels)


def body(inputs, queries, kv_weight, short_taps, filter_taps, skip_gain, out_weight):
    taps_all = lax.all_to_all(filter_taps, "ctx", split_axis=1, concat_axis=0, tiled=True)
    projected = jnp.einsum(
        "td,dkc->tkc", inputs, kv_weight, preferred_element_type=jnp.float32
    ).astype(jnp.bfloat16)
    carried = shifted(projected[-2:], "ctx", 1)
    extended = jnp.concatenate([carried, projected], 0).astype(jnp.float32)
    smoothed = (
        short_taps[0] * extended[2:]
        + short_taps[1] * extended[1:-1]
        + short_taps[2] * extended[:-2]
    )
    kv_product = (smoothed[:, 0] * smoothed[:, 1]).astype(jnp.bfloat16)
    kv_all = lax.all_to_all(kv_product, "ctx", split_axis=1, concat_axis=0, tiled=True)
    conv_all = local_conv(kv_all, taps_all)
    long_conv = lax.all_to_all(conv_all, "ctx", split_axis=0, concat_axis=1, tiled=True)
    gated = (
        queries.astype(jnp.float32)
        * (long_conv.astype(jnp.float32) + skip_gain[None, :] * kv_product.astype(jnp.float32))
    ).astype(jnp.bfloat16)
    return lax.psum_scatter(
        jnp.dot(gated, out_weight, preferred_element_type=jnp.float32).astype(jnp.bfloat16),
        "tp",
        scatter_dimension=0,
        tiled=True,
    )


def solution(mesh):
    return jax.shard_map(
        body,
        mesh=mesh,
        in_specs=(
            P("ctx", None),
            P("ctx", "tp"),
            P(None, None, "tp"),
            P(None, None, "tp"),
            P("ctx", "tp"),
            P("tp"),
            P("tp", None),
        ),
        out_specs=P(("ctx", "tp"), None),
        check_vma=False,
    )
```

time: 1400 us -> 326 us (0.23)
  matrix products: 556 us -> 39 us
  waiting for transfers between devices: 576 us -> 161 us
  local copies, waits for them, and re-layouts: 134 us -> 6.82 us
  Pallas kernels: 0 us -> 31.2 us
  other arithmetic: 32.2 us -> 6.96 us
  starting transfers between devices: 31.8 us -> 7.4 us
    dot_general x22 -> x0, matrix products: 518 us -> none  [the longest x18 461 us: contract(): return jnp.einsum(form, table, data, precision=lax.Precision.HIGHEST)]
    all_to_all x5 -> x1, waiting for transfers between devices: 432 us -> 16.5 us  [body(): lax.all_to_all(filter_taps, 'ctx', split_axis=1, concat_axis=0, tiled=True)]
    all_to_all x7 -> x1, local copies, waits for them, and re-layouts: 47.8 us -> 1.7 us  [body(): lax.all_to_all(filter_taps, 'ctx', split_axis=1, concat_axis=0, tiled=True)]
    reshape x3 -> x0, local copies, waits for them, and re-layouts: 32.3 us -> none  [the longest x2 26 us: inverse_steps(): return (out_real.reshape(shape_out), out_imag.reshape(shape_out))]
    pallas_call x0 -> x1, Pallas kernels: none -> 31.2 us  [local_conv(): pl.pallas_call(functools.partial(conv_kernel, half, per_step, 0.5 / lengt...]
    sub x2 -> x0, other arithmetic: 25.4 us -> none  [the longest x1 18.6 us: spread_conv(): prod_real = spec_real[0] * spec_real[1] - spec_imag[0] * spec_imag[1]]
    all_to_all x5 -> x1, starting transfers between devices: 29.2 us -> 5.01 us  [body(): lax.all_to_all(filter_taps, 'ctx', split_axis=1, concat_axis=0, tiled=True)]
    add x2 -> x0, local copies, waits for them, and re-layouts: 22.7 us -> none  [the longest x1 17.8 us: spread_conv(): turned_real = head_real * cos_t + head_imag * sin_t]
  transfers between devices with their start and end apart: 7 -> 3, of which waited for: 7 -> 2; matrix products, arithmetic and copies ran while one was open for 12% -> 3% of each run, Pallas kernels for 0% -> 0%
where the time goes in v1:
time: 326 us
  waiting for transfers between devices  161 us (49%)
  blocking collectives  60 us (18%)
  matrix products  39 us (12%)
  Pallas kernels  31.2 us (10%)
  between operations  13.5 us (4%)
  starting transfers between devices  7.4 us (2%)
  other arithmetic  6.96 us (2%)
  local copies, waits for them, and re-layouts  6.82 us (2%)
    reduce_scatter x1, waiting for transfers between devices, body(): lax.psum_scatter(jnp.dot(gated, out_weight, preferred_element_type=jnp.fl...  144 us
    pallas_call x1, Pallas kernels, local_conv(): pl.pallas_call(functools.partial(conv_kernel, half, per_step, 0.5 / lengt...  31.2 us
    all_to_all x1, blocking collectives, body(): lax.all_to_all(conv_all, 'ctx', split_axis=0, concat_axis=1, tiled=True)  30.2 us
    all_to_all x1, blocking collectives, body(): lax.all_to_all(kv_product, 'ctx', split_axis=1, concat_axis=0, tiled=True)  29.8 us
    dot_general x1, matrix products, body(): jnp.einsum('td,dkc->tkc', inputs, kv_weight, preferred_element_type=jnp.f...  23.2 us
    all_to_all x1, waiting for transfers between devices, body(): lax.all_to_all(filter_taps, 'ctx', split_axis=1, concat_axis=0, tiled=True)  16.5 us
    dot_general x1, matrix products, body(): jnp.dot(gated, out_weight, preferred_element_type=jnp.float32)  15.7 us
  transfers between devices with their start and end apart: 3, of which 2 were waited for; matrix products, arithmetic and copies ran while one was open for 3% of the time, Pallas kernels for 0%

profile of v1, /device:TPU:0, one launch (start us, length us, event | category | flops | bytes accessed | tf_op | source)
XLA Modules:
  0.0 325.5 jit_solution(5417862600800527120)
XLA Ops:
  6.5 0.0 copy-start
  6.5 23.2 %fusion.8 = bf16[1024,2,1024]{2,0,1:T(8,128)(2,1)S(1)} fusion(bf16[4096,2,1024]{2,1,0:T(2,128)(2,1)} %param.13, bf16[1024,4096]{1,0:T(8,128)(2,1)} %param.11), kind=kOutput, calls=%fused_computation.17 | convolution fusion | flops 17181966336 | bytes 29360128 | tf_op jit(solution)/shard_map/td,dkc->tkc/dot_general | solution.py:122
  29.8 0.0 copy-start.3
  29.8 1.9 copy-done.3
  31.7 0.0 copy-start.4
  31.8 2.4 collective-permute-start
  34.1 0.0 copy-done
  34.1 1.7 copy_bitcast_fusion
  35.8 5.0 %all-to-all-start.1 = ((bf16[1024,8,128]{2,0,1:T(8,128)(2,1)}), bf16[1024,8,128]{2,0,1:T(8,128)(2,1)}, u32[]{:S(2)}, u32[]{:S(2)}) async-start(bf16[1024,8,128]{2,0,1:T(8,128)(2,1)} %copy_bitcast_fusion), calls=%async_computation.1 | async-start | bytes 4194304 | tf_op jit(solution)/shard_map/all_to_all | solution.py:121
  40.8 0.0 reduce-scatter.2.cloned.1.call-start
  40.9 0.0 copy-done.4
  40.9 0.0 collective-permute-done
  40.9 3.4 %maximum_convert_fusion = f32[1026,2,1024]{2,0,1:T(8,128)S(1)} fusion(bf16[1024,2,1024]{2,0,1:T(8,128)(2,1)} %copy-done.3, bf16[2,2,1024]{2,0,1:T(2,128)(2,1)S(1)} %collective-permute-done), kind=kLoop, calls=%fused_computation.9 | loop fusion | flops 8404992 | bytes 12607488 | tf_op jit(solution)/shard_map/convert_element_type | solution.py:126
  44.3 2.5 fusion.2
  46.8 0.0 copy-start.2
  46.8 1.1 fusion.17
  47.9 2.2 copy-done.2
  50.1 0.6 copy.18
  50.8 0.3 copy.13
  51.1 16.5 %all-to-all-done.1 = bf16[1024,8,128]{2,0,1:T(8,128)(2,1)} async-done(((bf16[1024,8,128]{2,0,1:T(8,128)(2,1)}), bf16[1024,8,128]{2,0,1:T(8,128)(2,1)}, u32[]{:S(2)}, u32[]{:S(2)}) %all-to-all-start.1) | async-done | bytes 2097184 | tf_op jit(solution)/shard_map/all_to_all | solution.py:121
  67.6 29.8 %all_to_all.42 = bf16[1024,8,128]{2,0,1:T(8,128)(2,1)} all-to-all(bf16[1024,8,128]{2,0,1:T(8,128)(2,1)S(1)} %copy.13), channel_id=1, replica_groups=mesh['ctx'=8,'tp'=4] {'ctx'}, dimensions={1} | all-to-all | bytes 4194304 | tf_op jit(solution)/shard_map/all_to_all | solution.py:133
  97.4 31.2 %shard_map.109 = bf16[64,128,128]{2,1,0:T(8,128)(2,1)} custom-call(bf16[64,128,128]{2,1,0:T(8,128)(2,1)} %bitcast.48, bf16[64,128,128]{2,1,0:T(8,128)(2,1)} %bitcast.7.taps_ref, bf16[1040,512]{1,0:T(8,128)(2,1)} %constant.8.clone.first_ref, bf16[512,1040]{1,0:T(8,128)(2,1)} %constant.9.clone.last_ref, bf16[65,256,256]{2,1,0:T(8,128)(2,1)} %constant.10.clone.fwd_ref, ...), custom_call_target="tpu_custom_call" | custom-call | tf_op jit(solution)/shard_map/pallas_call | solution.py:105
  128.6 0.0 copy-start.5
  128.6 0.0 copy-start.6
  128.6 30.2 %all_to_all.43 = bf16[8,1024,128]{2,1,0:T(8,128)(2,1)S(1)} all-to-all(bf16[8,1024,128]{2,1,0:T(8,128)(2,1)} %bitcast.49), channel_id=1, replica_groups=mesh['ctx'=8,'tp'=4] {'ctx'}, dimensions={0} | all-to-all | bytes 4194304 | tf_op jit(solution)/shard_map/all_to_all | solution.py:135
  158.8 0.0 copy-done.5
  158.8 0.0 copy-done.6
  158.8 15.7 %convolution_convert_fusion = bf16[1024,4096]{1,0:T(8,128)(2,1)} fusion(bf16[1024,4096]{1,0:T(8,128)(2,1)} %param.17, bf16[1024,1024]{1,0:T(8,128)(2,1)S(1)} %copy-done.5, f32[1024]{0:T(1024)S(1)} %copy-done.6, bf16[8,1024,128]{2,1,0:T(8,128)(2,1)S(1)} %all_to_all.43, f32[1024,2,1024]{2,0,1:T(8,128)} %copy-done.2), kind=kOutput, calls=%fused_computation.8 | convolution fusion | flops 8603566080 | bytes 29364224 | tf_op jit(solution)/shard_map/dot_general | solution.py:141
  174.6 0.0 copy-start.1
  174.6 0.0 reduce-scatter.2.cloned.1.call-update
  174.6 144.1 %reduce-scatter.2.cloned.1.call-done = bf16[256,4096]{1,0:T(8,128)(2,1)} async-done(((bf16[1024,4096]{1,0:T(8,128)(2,1)}), bf16[256,4096]{1,0:T(8,128)(2,1)}) %reduce-scatter.2.cloned.1.call-update) | async-done | bytes 2097168 | tf_op jit(solution)/shard_map/reduce_scatter | solution.py:140
  318.7 0.0 copy-done.1
  (2 shorter events, 0.0 us)
Async XLA Ops:
  6.5 27.6 %copy-start = (bf16[1024,1024]{1,0:T(8,128)(2,1)S(1)}, bf16[1024,1024]{1,0:T(8,128)(2,1)}, u32[]{:S(2)}) copy-start(bf16[1024,1024]{1,0:T(8,128)(2,1)} %param.15) | copy-start | bytes 6291460
  29.8 2.0 copy-start.3
  31.7 9.1 %copy-start.4 = (f32[3,2,1024]{2,1,0:T(2,128)S(1)}, f32[3,2,1024]{2,1,0:T(2,128)}, u32[]{:S(2)}) copy-start(f32[3,2,1024]{2,1,0:T(2,128)} %param.14) | copy-start | bytes 73732
  31.8 9.2 %collective-permute-start = (bf16[2,2,1024]{2,0,1:T(2,128)(2,1)S(1)}, bf16[2,2,1024]{2,0,1:T(2,128)(2,1)S(1)}, u32[]{:S(2)}, u32[]{:S(2)}) collective-permute-start(bf16[2,2,1024]{2,0,1:T(2,128)(2,1)S(1)} %slice.36), channel_id=1, source_target_pairs={{0,4},{4,8},{8,12},{12,16},{16,20},{20,24},{24,28},{1,5},{5,9},{9,... | collective-permute-start | bytes 24584 | tf_op jit(solution)/shard_map/ppermute | solution.py:19
  35.8 31.8 %all-to-all-start.1 = ((bf16[1024,8,128]{2,0,1:T(8,128)(2,1)}), bf16[1024,8,128]{2,0,1:T(8,128)(2,1)}, u32[]{:S(2)}, u32[]{:S(2)}) async-start(bf16[1024,8,128]{2,0,1:T(8,128)(2,1)} %copy_bitcast_fusion), calls=%async_computation.1 | async-start | bytes 4194304 | tf_op jit(solution)/shard_map/all_to_all | solution.py:121
  40.8 277.8 %reduce-scatter.2.cloned.1.call-start = ((), (), s32[]{:S(2)}) async-start(), calls=%async_computation.4 | async-start | bytes 10485760 | tf_op jit(solution)/shard_map/reduce_scatter | solution.py:140
  46.8 3.3 %copy-start.2 = (f32[1024,2,1024]{2,0,1:T(8,128)}, f32[1024,2,1024]{2,0,1:T(8,128)S(1)}, u32[]{:S(2)}) copy-start(f32[1024,2,1024]{2,0,1:T(8,128)S(1)} %fusion.2) | copy-start | bytes 25165828
  128.6 30.3 %copy-start.5 = (bf16[1024,1024]{1,0:T(8,128)(2,1)S(1)}, bf16[1024,1024]{1,0:T(8,128)(2,1)}, u32[]{:S(2)}) copy-start(bf16[1024,1024]{1,0:T(8,128)(2,1)} %param.12) | copy-start | bytes 6291460
  128.6 30.3 %copy-start.6 = (f32[1024]{0:T(1024)S(1)}, f32[1024]{0:T(1024)}, u32[]{:S(2)}) copy-start(f32[1024]{0:T(1024)} %param.16) | copy-start | bytes 12292
  174.6 144.1 %copy-start.1 = (bf16[1024,1024]{1,0:T(8,128)(2,1)S(1)}, bf16[1024,1024]{1,0:T(8,128)(2,1)}, u32[]{:S(2)}) copy-start(bf16[1024,1024]{1,0:T(8,128)(2,1)} %param.15) | copy-start | bytes 6291460
Sparse Core Ops, SparseCore 0:
  174.7 143.9 reduce-scatter.1

commit v2 on v1

--- a/solution.py
+++ b/solution.py
@@ -118,10 +118,25 @@
 
 
 def body(inputs, queries, kv_weight, short_taps, filter_taps, skip_gain, out_weight):
+    groups, shards = lax.axis_size("tp"), lax.axis_size("ctx")
+    group, core = lax.axis_index("tp"), lax.axis_index("ctx") % 2
+    mates = [(d, d ^ 1) for d in range(groups)]
+    siblings = [(d, d ^ 1) for d in range(shards)]
+    half_rows = out_weight.shape[0] // 2
+    part_rows = half_rows // 2
+    fetched = [
+        lax.ppermute(
+            lax.dynamic_slice_in_dim(out_weight, core * half_rows + j * part_rows, part_rows, 0),
+            "tp",
+            mates,
+        )
+        for j in range(2)
+    ]
     taps_all = lax.all_to_all(filter_taps, "ctx", split_axis=1, concat_axis=0, tiled=True)
     projected = jnp.einsum(
         "td,dkc->tkc", inputs, kv_weight, preferred_element_type=jnp.float32
     ).astype(jnp.bfloat16)
+    projected, taps_all = lax.optimization_barrier((projected, taps_all))
     carried = shifted(projected[-2:], "ctx", 1)
     extended = jnp.concatenate([carried, projected], 0).astype(jnp.float32)
     smoothed = (
@@ -131,18 +146,39 @@
     )
     kv_product = (smoothed[:, 0] * smoothed[:, 1]).astype(jnp.bfloat16)
     kv_all = lax.all_to_all(kv_product, "ctx", split_axis=1, concat_axis=0, tiled=True)
+    kv_all, fetched[0] = lax.optimization_barrier((kv_all, fetched[0]))
     conv_all = local_conv(kv_all, taps_all)
+    conv_all, fetched[1] = lax.optimization_barrier((conv_all, fetched[1]))
+    passed = [lax.ppermute(part, "ctx", siblings) for part in fetched]
     long_conv = lax.all_to_all(conv_all, "ctx", split_axis=0, concat_axis=1, tiled=True)
     gated = (
         queries.astype(jnp.float32)
         * (long_conv.astype(jnp.float32) + skip_gain[None, :] * kv_product.astype(jnp.float32))
     ).astype(jnp.bfloat16)
-    return lax.psum_scatter(
-        jnp.dot(gated, out_weight, preferred_element_type=jnp.float32).astype(jnp.bfloat16),
-        "tp",
-        scatter_dimension=0,
-        tiled=True,
+    mate_weight = jnp.concatenate(fetched + passed, 0)
+    turned = jnp.where(
+        core == 0, gated, jnp.concatenate([gated[:, half_rows:], gated[:, :half_rows]], 1)
     )
+    rows = gated.shape[0] // groups
+
+    def chunk(array, index):
+        return lax.dynamic_slice_in_dim(array, index % groups * rows, rows, 0)
+
+    steps = list(range(2, groups, 2)) + [0]
+    received = {
+        step: lax.ppermute(chunk(turned, (group ^ 1) + step), "tp", mates) for step in steps
+    }
+    arrived = []
+    for step in steps:
+        part = jnp.dot(
+            chunk(gated, group + step), out_weight, preferred_element_type=jnp.float32
+        ) + jnp.dot(received[step], mate_weight, preferred_element_type=jnp.float32)
+        if step:
+            ring = [(d, (d + step) % groups) for d in range(groups)]
+            arrived.append(lax.ppermute(part.astype(jnp.bfloat16), "tp", ring))
+    for other in arrived:
+        part = part + other.astype(jnp.float32)
+    return part.astype(jnp.bfloat16)
 
 
 def solution(mesh):

time: 326 us -> 281 us (0.86)
  blocking collectives: 60 us -> 0 us
  waiting for transfers between devices: 161 us -> 128 us
  local copies, waits for them, and re-layouts: 6.82 us -> 29.4 us
  starting transfers between devices: 7.4 us -> 25.3 us
  between operations: 13.5 us -> 0.24 us
  matrix products: 39 us -> 50.4 us
  other arithmetic: 6.96 us -> 13.7 us
    reduce_scatter x1 -> x0, waiting for transfers between devices: 144 us -> none  [body(): lax.psum_scatter(jnp.dot(gated, out_weight, preferred_element_type=jnp.fl...]
    ppermute x0 -> x7, waiting for transfers between devices: none -> 82.7 us  [the longest x2 46.9 us: body(): lax.ppermute(chunk(turned, (group ^ 1) + step), 'tp', mates)]
    all_to_all x2 -> x0, blocking collectives: 60 us -> none  [the longest x1 30.2 us: body(): lax.all_to_all(conv_all, 'ctx', split_axis=0, concat_axis=1, tiled=True)]
    all_to_all x0 -> x2, waiting for transfers between devices: none -> 44.8 us  [the longest x1 25.3 us: body(): lax.all_to_all(kv_product, 'ctx', split_axis=1, concat_axis=0, tiled=True)]
    all_to_all x1, waiting for transfers between devices: 16.5 us -> 0.01 us  [body(): lax.all_to_all(filter_taps, 'ctx', split_axis=1, concat_axis=0, tiled=True)]
    unnamed x15, local copies, waits for them, and re-layouts: 4.83 us -> 16.5 us
    all_to_all x0 -> x2, starting transfers between devices: none -> 11 us  [the longest x1 6.51 us: body(): lax.all_to_all(kv_product, 'ctx', split_axis=1, concat_axis=0, tiled=True)]
    dot_general x1 -> x4, matrix products: 15.7 us -> 26.5 us  [the longest x2 15.1 us: body(): jnp.dot(received[step], mate_weight, preferred_element_type=jnp.float32)]
  transfers between devices with their start and end apart: 3 -> 11, of which waited for: 2 -> 6; matrix products, arithmetic and copies ran while one was open for 3% -> 25% of each run, Pallas kernels for 0% -> 11%
where the time goes in v2:
time: 281 us; the launch traced here: 279 us
  waiting for transfers between devices  128 us (46%)
  matrix products  50.4 us (18%)
  Pallas kernels  31.3 us (11%)
  local copies, waits for them, and re-layouts  29.4 us (10%)
  starting transfers between devices  25.3 us (9%)
  other arithmetic  13.7 us (5%)
    ppermute x2, waiting for transfers between devices, body(): lax.ppermute(chunk(turned, (group ^ 1) + step), 'tp', mates)  46.9 us
    ppermute x1, waiting for transfers between devices, body(): arrived.append(lax.ppermute(part.astype(jnp.bfloat16), 'tp', ring))  34.5 us
    pallas_call x1, Pallas kernels, local_conv(): pl.pallas_call(functools.partial(conv_kernel, half, per_step, 0.5 / lengt...  31.3 us
    all_to_all x1, waiting for transfers between devices, body(): lax.all_to_all(kv_product, 'ctx', split_axis=1, concat_axis=0, tiled=True)  25.3 us
    dot_general x1, matrix products, body(): jnp.einsum('td,dkc->tkc', inputs, kv_weight, preferred_element_type=jnp.f...  23.9 us
    all_to_all x1, waiting for transfers between devices, body(): lax.all_to_all(conv_all, 'ctx', split_axis=0, concat_axis=1, tiled=True)  19.5 us
    unnamed x15, local copies, waits for them, and re-layouts  16.5 us
    dot_general x2, matrix products, body(): jnp.dot(received[step], mate_weight, preferred_element_type=jnp.float32)  15.1 us
  transfers between devices with their start and end apart: 11, of which 6 were waited for; matrix products, arithmetic and copies ran while one was open for 25% of the time, Pallas kernels for 11%

profile of v2, /device:TPU:0, one launch (start us, length us, event | category | flops | bytes accessed | tf_op | source)
XLA Modules:
  0.0 278.6 jit_solution(12230076968801148587)
XLA Ops:
  0.0 2.9 %copy.20 = bf16[1024,1024]{0,1:T(8,128)(2,1)S(1)} copy(bf16[1024,1024]{1,0:T(8,128)(2,1)} %param.15) | data formatting | bytes 4194304 | tf_op args[4]
  2.9 2.4 copy.21
  5.2 5.2 %all-to-all-start = ((bf16[1024,8,128]{2,0,1:T(8,128)(2,1)}), bf16[1024,8,128]{2,0,1:T(8,128)(2,1)S(1)}, u32[]{:S(2)}, u32[]{:S(2)}) async-start(bf16[1024,8,128]{2,0,1:T(8,128)(2,1)} %copy.21), calls=%async_computation | async-start | bytes 4194304 | tf_op jit(solution)/shard_map/all_to_all | solution.py:135
  10.4 4.7 %constant_dynamic-slice_fusion.2 = (bf16[256,4096]{1,0:T(8,128)(2,1)}, bf16[256,4096]{1,0:T(8,128)(2,1)}) fusion(bf16[1024,4096]{1,0:T(8,128)(2,1)} %param.17, s32[]{:T(128)S(6)} %select_n.51, s32[]{:T(128)S(6)} %select_n.50), kind=kLoop, calls=%fused_computation.38 | loop fusion | bytes 8388616 | tf_op jit(solution)/shard_map/dynamic_slice | solution.py:129
  15.1 1.6 collective-permute-start.1
  17.1 23.9 %fusion.11 = bf16[1024,2,1024]{2,0,1:T(8,128)(2,1)} fusion(bf16[4096,2,1024]{2,1,0:T(2,128)(2,1)} %param.13, bf16[1024,4096]{1,0:T(8,128)(2,1)} %param.11), kind=kOutput, calls=%fused_computation.21 | convolution fusion | flops 17181966336 | bytes 29360128 | tf_op jit(solution)/shard_map/td,dkc->tkc/dot_general | solution.py:136
  41.8 1.9 collective-permute-start
  44.5 3.4 %maximum_convert_fusion = f32[1026,2,1024]{2,0,1:T(8,128)S(1)} fusion(bf16[1024,2,1024]{2,0,1:T(8,128)(2,1)} %fusion.11, bf16[2,2,1024]{2,0,1:T(2,128)(2,1)S(1)} %collective-permute-done), kind=kLoop, calls=%fused_computation.13 | loop fusion | flops 8404992 | bytes 12607488 | tf_op jit(solution)/shard_map/convert_element_type | solution.py:141
  47.9 2.5 fusion.2
  50.4 1.1 fusion.29
  51.4 2.3 copy-done
  54.3 1.7 copy.22
  56.0 6.5 %all-to-all-start.1 = ((bf16[1024,8,128]{2,0,1:T(8,128)(2,1)}), bf16[1024,8,128]{2,0,1:T(8,128)(2,1)S(1)}, u32[]{:S(2)}, u32[]{:S(2)}) async-start(bf16[1024,8,128]{2,0,1:T(8,128)(2,1)} %copy.22), calls=%async_computation.1 | async-start | bytes 4194304 | tf_op jit(solution)/shard_map/all_to_all | solution.py:148
  62.5 1.4 collective-permute-done.1
  63.8 25.3 %all-to-all-done.1 = bf16[1024,8,128]{2,0,1:T(8,128)(2,1)S(1)} async-done(((bf16[1024,8,128]{2,0,1:T(8,128)(2,1)}), bf16[1024,8,128]{2,0,1:T(8,128)(2,1)S(1)}, u32[]{:S(2)}, u32[]{:S(2)}) %all-to-all-start.1) | async-done | bytes 2097184 | tf_op jit(solution)/shard_map/all_to_all | solution.py:148
  89.1 1.3 copy-done.2
  90.5 31.3 %shard_map.109 = bf16[64,128,128]{2,1,0:T(8,128)(2,1)} custom-call(bf16[64,128,128]{2,1,0:T(8,128)(2,1)} %bitcast.50, bf16[64,128,128]{2,1,0:T(8,128)(2,1)} %bitcast.49, bf16[1040,512]{1,0:T(8,128)(2,1)} %constant.62.clone.first_ref, bf16[512,1040]{1,0:T(8,128)(2,1)} %constant.63.clone.last_ref, bf16[65,256,256]{2,1,0:T(8,128)(2,1)} %constant.64.clone.fwd_ref, ...), custom_call_target="tpu_custom_call" | custom-call | tf_op jit(solution)/shard_map/pallas_call | solution.py:105
  121.7 4.5 %all-to-all-start.2 = ((bf16[8,1024,128]{2,1,0:T(8,128)(2,1)}), bf16[8,1024,128]{2,1,0:T(8,128)(2,1)}, u32[]{:S(2)}, u32[]{:S(2)}) async-start(bf16[8,1024,128]{2,1,0:T(8,128)(2,1)} %bitcast.48), calls=%async_computation.2 | async-start | bytes 4194304 | tf_op jit(solution)/shard_map/all_to_all | solution.py:153
  126.9 3.2 %constant_dynamic-update-slice_fusion.3 = bf16[1024,4096]{1,0:T(8,128)(2,1)} fusion(bf16[256,4096]{1,0:T(8,128)(2,1)} %collective-permute-done.1), kind=kLoop, calls=%fused_computation.30 | loop fusion | bytes 4194304
  130.1 3.1 %constant_dynamic-update-slice_fusion.2 = bf16[1024,4096]{1,0:T(8,128)(2,1)} fusion(bf16[1024,4096]{1,0:T(8,128)(2,1)} %constant_dynamic-update-slice_fusion.3, bf16[256,4096]{1,0:T(8,128)(2,1)} %collective-permute-done.2), kind=kLoop, calls=%fused_computation.29 | loop fusion | bytes 4194304
  133.3 19.5 %all-to-all-done.2 = bf16[8,1024,128]{2,1,0:T(8,128)(2,1)} async-done(((bf16[8,1024,128]{2,1,0:T(8,128)(2,1)}), bf16[8,1024,128]{2,1,0:T(8,128)(2,1)}, u32[]{:S(2)}, u32[]{:S(2)}) %all-to-all-start.2) | async-done | bytes 2097184 | tf_op jit(solution)/shard_map/all_to_all | solution.py:153
  152.8 6.0 %fusion.9 = bf16[1024,1024]{1,0:T(8,128)(2,1)S(1)} fusion(bf16[1024,1024]{1,0:T(8,128)(2,1)} %param.12, f32[1024]{0:T(1024)S(1)} %copy-done.4, f32[1024,2,1024]{2,0,1:T(8,128)} %copy-done, bf16[8,1024,128]{2,1,0:T(8,128)(2,1)} %all-to-all-done.2), kind=kLoop, calls=%fused_computation.16 | loop fusion | flops 9437184 | bytes 14684160 | tf_op jit(solution)/shard_map/convert_element_type | solution.py:157
  159.8 1.6 collective-permute-start.6
  161.4 5.7 %fusion.16 = f32[256,4096]{1,0:T(8,128)S(1)} fusion(bf16[1024,4096]{1,0:T(8,128)(2,1)} %param.17, bf16[1024,1024]{1,0:T(8,128)(2,1)S(1)} %fusion.9, s32[]{:T(128)S(6)} %select_n.59), kind=kOutput, calls=%fused_computation.23 | convolution fusion | flops 2147483648 | bytes 13107204 | tf_op jit(solution)/shard_map/dot_general | solution.py:173
  167.1 3.1 %constant_dynamic-update-slice_fusion.1 = bf16[1024,4096]{1,0:T(8,128)(2,1)} fusion(bf16[1024,4096]{1,0:T(8,128)(2,1)} %constant_dynamic-update-slice_fusion.2, bf16[256,4096]{1,0:T(8,128)(2,1)} %collective-permute-done.4), kind=kLoop, calls=%fused_computation.28 | loop fusion | bytes 4194304
  170.3 3.1 %constant_dynamic-update-slice_fusion = bf16[1024,4096]{1,0:T(8,128)(2,1)} fusion(bf16[1024,4096]{1,0:T(8,128)(2,1)} %constant_dynamic-update-slice_fusion.1, bf16[256,4096]{1,0:T(8,128)(2,1)} %collective-permute-done.5), kind=kLoop, calls=%fused_computation.27 | loop fusion | bytes 4194304 | tf_op jit(solution)/shard_map/concatenate | solution.py:158
  173.4 7.2 %fusion.7 = bf16[256,4096]{1,0:T(8,128)(2,1)} fusion(f32[256,4096]{1,0:T(8,128)S(1)} %fusion.16, bf16[256,1024]{1,0:T(8,128)(2,1)S(1)} %collective-permute-done.6, bf16[1024,4096]{1,0:T(8,128)(2,1)} %constant_dynamic-update-slice_fusion), kind=kOutput, calls=%fused_computation.12 | convolution fusion | flops 2149580800 | bytes 15204352 | tf_op jit(solution)/shard_map/dot_general | solution.py:175
  180.6 2.6 collective-permute-start.7
  183.6 5.7 %fusion.18 = f32[256,4096]{1,0:T(8,128)S(1)} fusion(bf16[1024,4096]{1,0:T(8,128)(2,1)} %param.17, bf16[1024,1024]{1,0:T(8,128)(2,1)S(1)} %fusion.9, s32[]{:T(128)S(6)} %select_n.53), kind=kOutput, calls=%fused_computation.25 | convolution fusion | flops 2147483648 | bytes 13107204 | tf_op jit(solution)/shard_map/dot_general | solution.py:173
  189.3 46.9 %collective-permute-done.3 = bf16[256,1024]{1,0:T(8,128)(2,1)S(1)} collective-permute-done((bf16[256,1024]{1,0:T(8,128)(2,1)S(1)}, bf16[256,1024]{1,0:T(8,128)(2,1)S(1)}, u32[]{:S(2)}, u32[]{:S(2)}) %collective-permute-start.3) | collective-permute-done | bytes 524320 | tf_op jit(solution)/shard_map/ppermute | solution.py:169
  236.2 34.5 %collective-permute-done.7 = bf16[256,4096]{1,0:T(8,128)(2,1)} collective-permute-done((bf16[256,4096]{1,0:T(8,128)(2,1)}, bf16[256,4096]{1,0:T(8,128)(2,1)}, u32[]{:S(2)}, u32[]{:S(2)}) %collective-permute-start.7) | collective-permute-done | bytes 2097184 | tf_op jit(solution)/shard_map/ppermute | solution.py:178
  270.7 7.9 %fusion.6 = bf16[256,4096]{1,0:T(8,128)(2,1)} fusion(f32[256,4096]{1,0:T(8,128)S(1)} %fusion.18, bf16[256,1024]{1,0:T(8,128)(2,1)S(1)} %collective-permute-done.3, bf16[1024,4096]{1,0:T(8,128)(2,1)} %constant_dynamic-update-slice_fusion, bf16[256,4096]{1,0:T(8,128)(2,1)} %collective-permute-done.7), kind=kOutput, calls=%fused_computation.11 | convolution fusion | flops 2151677952 | bytes 17301504 | tf_op jit(solution)/shard_map/dot_general | solution.py:175
  (24 shorter events, 4.7 us)
Async XLA Ops:
  5.2 35.8 %all-to-all-start = ((bf16[1024,8,128]{2,0,1:T(8,128)(2,1)}), bf16[1024,8,128]{2,0,1:T(8,128)(2,1)S(1)}, u32[]{:S(2)}, u32[]{:S(2)}) async-start(bf16[1024,8,128]{2,0,1:T(8,128)(2,1)} %copy.21), calls=%async_computation | async-start | bytes 4194304 | tf_op jit(solution)/shard_map/all_to_all | solution.py:135
  15.1 48.7 %collective-permute-start.1 = (bf16[256,4096]{1,0:T(8,128)(2,1)}, bf16[256,4096]{1,0:T(8,128)(2,1)}, u32[]{:S(2)}, u32[]{:S(2)}) collective-permute-start(bf16[256,4096]{1,0:T(8,128)(2,1)} %get-tuple-element.18), channel_id=1, source_target_pairs={{0,1},{1,0},{2,3},{3,2},{4,5},{5,4},{6,7},{7,6},{8,9},{9,8},{10,11... | collective-permute-start | bytes 6291464 | tf_op jit(solution)/shard_map/ppermute | solution.py:128
  16.7 27.0 %copy-start.3 = (f32[3,2,1024]{2,1,0:T(2,128)S(1)}, f32[3,2,1024]{2,1,0:T(2,128)}, u32[]{:S(2)}) copy-start(f32[3,2,1024]{2,1,0:T(2,128)} %param.14) | copy-start | bytes 73732
  16.7 105.0 %collective-permute-start.2 = (bf16[256,4096]{1,0:T(8,128)(2,1)}, bf16[256,4096]{1,0:T(8,128)(2,1)}, u32[]{:S(2)}, u32[]{:S(2)}) collective-permute-start(bf16[256,4096]{1,0:T(8,128)(2,1)} %get-tuple-element.17), channel_id=1, source_target_pairs={{0,1},{1,0},{2,3},{3,2},{4,5},{5,4},{6,7},{7,6},{8,9},{9,8},{10,11... | collective-permute-start | bytes 6291464 | tf_op jit(solution)/shard_map/ppermute | solution.py:128
  41.0 6.9 %copy-start.1 = (bf16[1024,8,128]{2,0,1:T(8,128)(2,1)}, bf16[1024,8,128]{2,0,1:T(8,128)(2,1)S(1)}, u32[]{:S(2)}) copy-start(bf16[1024,8,128]{2,0,1:T(8,128)(2,1)S(1)} %all-to-all-done) | copy-start | bytes 6291460
  41.8 2.7 collective-permute-start
  50.4 3.3 %copy-start = (f32[1024,2,1024]{2,0,1:T(8,128)}, f32[1024,2,1024]{2,0,1:T(8,128)S(1)}, u32[]{:S(2)}) copy-start(f32[1024,2,1024]{2,0,1:T(8,128)S(1)} %fusion.2) | copy-start | bytes 25165828
  56.0 33.2 %all-to-all-start.1 = ((bf16[1024,8,128]{2,0,1:T(8,128)(2,1)}), bf16[1024,8,128]{2,0,1:T(8,128)(2,1)S(1)}, u32[]{:S(2)}, u32[]{:S(2)}) async-start(bf16[1024,8,128]{2,0,1:T(8,128)(2,1)} %copy.22), calls=%async_computation.1 | async-start | bytes 4194304 | tf_op jit(solution)/shard_map/all_to_all | solution.py:148
  89.1 1.3 copy-start.2
  121.7 31.0 %all-to-all-start.2 = ((bf16[8,1024,128]{2,1,0:T(8,128)(2,1)}), bf16[8,1024,128]{2,1,0:T(8,128)(2,1)}, u32[]{:S(2)}, u32[]{:S(2)}) async-start(bf16[8,1024,128]{2,1,0:T(8,128)(2,1)} %bitcast.48), calls=%async_computation.2 | async-start | bytes 4194304 | tf_op jit(solution)/shard_map/all_to_all | solution.py:153
  126.3 26.4 %copy-start.4 = (f32[1024]{0:T(1024)S(1)}, f32[1024]{0:T(1024)}, u32[]{:S(2)}) copy-start(f32[1024]{0:T(1024)} %param.16) | copy-start | bytes 12292
  126.4 40.8 %collective-permute-start.4 = (bf16[256,4096]{1,0:T(8,128)(2,1)}, bf16[256,4096]{1,0:T(8,128)(2,1)}, u32[]{:S(2)}, u32[]{:S(2)}) collective-permute-start(bf16[256,4096]{1,0:T(8,128)(2,1)} %collective-permute-done.1), channel_id=1, source_target_pairs={{0,4},{4,0},{8,12},{12,8},{16,20},{20,16},{24,28},{28,24},{1,5},{5... | collective-permute-start | bytes 6291464 | tf_op jit(solution)/shard_map/ppermute | solution.py:152
  126.5 43.8 %collective-permute-start.5 = (bf16[256,4096]{1,0:T(8,128)(2,1)}, bf16[256,4096]{1,0:T(8,128)(2,1)}, u32[]{:S(2)}, u32[]{:S(2)}) collective-permute-start(bf16[256,4096]{1,0:T(8,128)(2,1)} %collective-permute-done.2), channel_id=1, source_target_pairs={{0,4},{4,0},{8,12},{12,8},{16,20},{20,16},{24,28},{28,24},{1,5},{5... | collective-permute-start | bytes 6291464 | tf_op jit(solution)/shard_map/ppermute | solution.py:152
  159.8 13.6 %collective-permute-start.6 = (bf16[256,1024]{1,0:T(8,128)(2,1)S(1)}, bf16[256,1024]{1,0:T(8,128)(2,1)S(1)}, u32[]{:S(2)}, u32[]{:S(2)}) collective-permute-start(bf16[256,1024]{1,0:T(8,128)(2,1)S(1)} %get-tuple-element.19), channel_id=1, source_target_pairs={{0,1},{1,0},{2,3},{3,2},{4,5},{5,4},{6,7},{7,6},{8,9},{9,8},{10,11... | collective-permute-start | bytes 1572872 | tf_op jit(solution)/shard_map/ppermute | solution.py:169
  180.6 90.1 %collective-permute-start.7 = (bf16[256,4096]{1,0:T(8,128)(2,1)}, bf16[256,4096]{1,0:T(8,128)(2,1)}, u32[]{:S(2)}, u32[]{:S(2)}) collective-permute-start(bf16[256,4096]{1,0:T(8,128)(2,1)} %fusion.7), channel_id=1, source_target_pairs={{0,2},{1,3},{2,0},{3,1},{4,6},{5,7},{6,4},{7,5},{8,10},{9,11},{10,... | collective-permute-start | bytes 6291464 | tf_op jit(solution)/shard_map/ppermute | solution.py:178
  183.2 53.0 %collective-permute-start.3 = (bf16[256,1024]{1,0:T(8,128)(2,1)S(1)}, bf16[256,1024]{1,0:T(8,128)(2,1)S(1)}, u32[]{:S(2)}, u32[]{:S(2)}) collective-permute-start(bf16[256,1024]{1,0:T(8,128)(2,1)S(1)} %get-tuple-element.20), channel_id=1, source_target_pairs={{0,1},{1,0},{2,3},{3,2},{4,5},{5,4},{6,7},{7,6},{8,9},{9,8},{10,11... | collective-permute-start | bytes 1572872 | tf_op jit(solution)/shard_map/ppermute | solution.py:169

commit v3 on v2

--- a/solution.py
+++ b/solution.py
@@ -150,35 +150,47 @@
     conv_all = local_conv(kv_all, taps_all)
     conv_all, fetched[1] = lax.optimization_barrier((conv_all, fetched[1]))
     passed = [lax.ppermute(part, "ctx", siblings) for part in fetched]
-    long_conv = lax.all_to_all(conv_all, "ctx", split_axis=0, concat_axis=1, tiled=True)
-    gated = (
-        queries.astype(jnp.float32)
-        * (long_conv.astype(jnp.float32) + skip_gain[None, :] * kv_product.astype(jnp.float32))
-    ).astype(jnp.bfloat16)
     mate_weight = jnp.concatenate(fetched + passed, 0)
-    turned = jnp.where(
-        core == 0, gated, jnp.concatenate([gated[:, half_rows:], gated[:, :half_rows]], 1)
-    )
-    rows = gated.shape[0] // groups
-
-    def chunk(array, index):
-        return lax.dynamic_slice_in_dim(array, index % groups * rows, rows, 0)
-
-    steps = list(range(2, groups, 2)) + [0]
-    received = {
-        step: lax.ppermute(chunk(turned, (group ^ 1) + step), "tp", mates) for step in steps
-    }
+    channels = conv_all.shape[1]
+    rows = queries.shape[0] // groups
+    conv_all = conv_all.reshape(shards, groups * rows, channels)
+    side = group % 2
+
+    def pair_rows(array, step, dim):
+        start = (group - side + step) % groups * rows
+        return lax.dynamic_slice_in_dim(array, start, 2 * rows, dim)
+
+    def pair_sum(conv_part, step):
+        conv_part = conv_part.reshape(shards * 2 * rows, channels)
+        long_conv = lax.all_to_all(conv_part, "ctx", split_axis=0, concat_axis=1, tiled=True)
+        gated = (
+            pair_rows(queries, step, 0).astype(jnp.float32)
+            * (
+                long_conv.astype(jnp.float32)
+                + skip_gain[None, :] * pair_rows(kv_product, step, 0).astype(jnp.float32)
+            )
+        ).astype(jnp.bfloat16)
+        sent = lax.dynamic_slice_in_dim(gated, (1 - side) * rows, rows, 0)
+        sent = jnp.where(
+            core == 0, sent, jnp.concatenate([sent[:, half_rows:], sent[:, :half_rows]], 1)
+        )
+        received = lax.ppermute(sent, "tp", mates)
+        own = lax.dynamic_slice_in_dim(gated, side * rows, rows, 0)
+        return jnp.dot(own, out_weight, preferred_element_type=jnp.float32) + jnp.dot(
+            received, mate_weight, preferred_element_type=jnp.float32
+        )
+
     arrived = []
-    for step in steps:
-        part = jnp.dot(
-            chunk(gated, group + step), out_weight, preferred_element_type=jnp.float32
-        ) + jnp.dot(received[step], mate_weight, preferred_element_type=jnp.float32)
-        if step:
-            ring = [(d, (d + step) % groups) for d in range(groups)]
-            arrived.append(lax.ppermute(part.astype(jnp.bfloat16), "tp", ring))
+    for step in range(2, groups, 2):
+        part = pair_sum(pair_rows(conv_all, step, 1), step).astype(jnp.bfloat16)
+        part, conv_all = lax.optimization_barrier((part, conv_all))
+        ring = [(d, (d + step) % groups) for d in range(groups)]
+        arrived.append(lax.ppermute(part, "tp", ring))
+    total = pair_sum(pair_rows(conv_all, 0, 1), 0)
+    total, *arrived = lax.optimization_barrier((total, *arrived))
     for other in arrived:
-        part = part + other.astype(jnp.float32)
-    return part.astype(jnp.bfloat16)
+        total = total + other.astype(jnp.float32)
+    return total.astype(jnp.bfloat16)
 
 
 def solution(mesh):

time: 281 us -> 268 us (0.954)
  waiting for transfers between devices: 128 us -> 109 us
  other arithmetic: 13.7 us -> 18.5 us
  starting transfers between devices: 25.3 us -> 28.2 us
    ppermute x3, waiting for transfers between devices: 81.3 us -> 64.6 us  [the longest x2 36 us: pair_sum(): received = lax.ppermute(sent, 'tp', mates)]
    convert_element_type x1 -> x4, other arithmetic: 5.99 us -> 11.2 us  [the longest x1 4.18 us: body(): kv_product = (smoothed[:, 0] * smoothed[:, 1]).astype(jnp.bfloat16)]
    dynamic_slice x1 -> x2, local copies, waits for them, and re-layouts: 0.08 us -> 3.35 us  [pair_rows(): return lax.dynamic_slice_in_dim(array, start, 2 * rows, dim)]
    all_to_all x1 -> x2, starting transfers between devices: 4.54 us -> 7.3 us  [pair_sum(): lax.all_to_all(conv_part, 'ctx', split_axis=0, concat_axis=1, tiled=True)]
    all_to_all x1 -> x2, waiting for transfers between devices: 19.5 us -> 21 us  [pair_sum(): lax.all_to_all(conv_part, 'ctx', split_axis=0, concat_axis=1, tiled=True)]
  transfers between devices with their start and end apart: 11 -> 12, of which waited for: 6 -> 6; matrix products, arithmetic and copies ran while one was open for 25% -> 29% of each run, Pallas kernels for 11% -> 12%
where the time goes in v3:
time: 268 us; the launch traced here: 267 us
  waiting for transfers between devices  109 us (41%)
  matrix products  48.6 us (18%)
  local copies, waits for them, and re-layouts  31.2 us (12%)
  Pallas kernels  31.2 us (12%)
  starting transfers between devices  28.2 us (11%)
  other arithmetic  18.5 us (7%)
    ppermute x2, waiting for transfers between devices, pair_sum(): received = lax.ppermute(sent, 'tp', mates)  36 us
    pallas_call x1, Pallas kernels, local_conv(): pl.pallas_call(functools.partial(conv_kernel, half, per_step, 0.5 / lengt...  31.2 us
    ppermute x1, waiting for transfers between devices, body(): arrived.append(lax.ppermute(part, 'tp', ring))  28.5 us
    dot_general x1, matrix products, body(): jnp.einsum('td,dkc->tkc', inputs, kv_weight, preferred_element_type=jnp.f...  23.8 us
    all_to_all x1, waiting for transfers between devices, body(): lax.all_to_all(kv_product, 'ctx', split_axis=1, concat_axis=0, tiled=True)  22.6 us
    all_to_all x2, waiting for transfers between devices, pair_sum(): lax.all_to_all(conv_part, 'ctx', split_axis=0, concat_axis=1, tiled=True)  21 us
    unnamed x15, local copies, waits for them, and re-layouts  15.1 us
    dot_general x2, matrix products, pair_sum(): jnp.dot(received, mate_weight, preferred_element_type=jnp.float32)  13.3 us
  transfers between devices with their start and end apart: 12, of which 6 were waited for; matrix products, arithmetic and copies ran while one was open for 29% of the time, Pallas kernels for 12%

profile of v3, /device:TPU:0, one launch (start us, length us, event | category | flops | bytes accessed | tf_op | source)
XLA Modules:
  0.0 266.8 jit_solution(9169418778470314671)
XLA Ops:
  0.0 2.9 %copy.22 = bf16[1024,1024]{0,1:T(8,128)(2,1)S(1)} copy(bf16[1024,1024]{1,0:T(8,128)(2,1)} %param.15) | data formatting | bytes 4194304 | tf_op args[4]
  2.9 2.4 copy.23
  5.2 5.2 %all-to-all-start = ((bf16[1024,8,128]{2,0,1:T(8,128)(2,1)}), bf16[1024,8,128]{2,0,1:T(8,128)(2,1)S(1)}, u32[]{:S(2)}, u32[]{:S(2)}) async-start(bf16[1024,8,128]{2,0,1:T(8,128)(2,1)} %copy.23), calls=%async_computation | async-start | bytes 4194304 | tf_op jit(solution)/shard_map/all_to_all | solution.py:135
  10.4 4.7 %constant_dynamic-slice_fusion.2 = (bf16[256,4096]{1,0:T(8,128)(2,1)}, bf16[256,4096]{1,0:T(8,128)(2,1)}) fusion(bf16[1024,4096]{1,0:T(8,128)(2,1)} %param.17, s32[]{:T(128)S(6)} %select_n.70, s32[]{:T(128)S(6)} %select_n.69), kind=kLoop, calls=%fused_computation.43 | loop fusion | bytes 8388616 | tf_op jit(solution)/shard_map/dynamic_slice | solution.py:129
  17.1 23.8 %fusion.7 = bf16[1024,2,1024]{2,0,1:T(8,128)(2,1)} fusion(bf16[4096,2,1024]{2,1,0:T(2,128)(2,1)} %param.13, bf16[1024,4096]{1,0:T(8,128)(2,1)} %param.11), kind=kOutput, calls=%fused_computation.15 | convolution fusion | flops 17181966336 | bytes 29360128 | tf_op jit(solution)/shard_map/td,dkc->tkc/dot_general | solution.py:136
  41.7 1.9 collective-permute-start
  44.4 3.4 %maximum_convert_fusion = f32[1026,2,1024]{2,0,1:T(8,128)S(1)} fusion(bf16[1024,2,1024]{2,0,1:T(8,128)(2,1)} %fusion.7, bf16[2,2,1024]{2,0,1:T(2,128)(2,1)S(1)} %collective-permute-done), kind=kLoop, calls=%fused_computation.11 | loop fusion | flops 8404992 | bytes 12607488 | tf_op jit(solution)/shard_map/convert_element_type | solution.py:141
  47.8 2.5 fusion.2
  51.4 2.3 copy-done
  55.9 6.5 %all-to-all-start.1 = ((bf16[1024,8,128]{2,0,1:T(8,128)(2,1)}), bf16[1024,8,128]{2,0,1:T(8,128)(2,1)}, u32[]{:S(2)}, u32[]{:S(2)}) async-start(bf16[1024,8,128]{2,0,1:T(8,128)(2,1)} %copy.24), calls=%async_computation.1 | async-start | bytes 4194304 | tf_op jit(solution)/shard_map/all_to_all | solution.py:148
  62.4 4.2 %fusion.6 = bf16[1024,1,1024]{2,0,1:T(8,128)(2,1)S(1)} fusion(f32[1024,2,1024]{2,0,1:T(8,128)} %copy-done), kind=kLoop, calls=%fused_computation.13 | loop fusion | flops 2097152 | bytes 10485760 | tf_op jit(solution)/shard_map/convert_element_type | solution.py:147
  66.6 22.6 %all-to-all-done.1 = bf16[1024,8,128]{2,0,1:T(8,128)(2,1)} async-done(((bf16[1024,8,128]{2,0,1:T(8,128)(2,1)}), bf16[1024,8,128]{2,0,1:T(8,128)(2,1)}, u32[]{:S(2)}, u32[]{:S(2)}) %all-to-all-start.1) | async-done | bytes 2097184 | tf_op jit(solution)/shard_map/all_to_all | solution.py:148
  89.2 31.2 %shard_map.109 = bf16[64,128,128]{2,1,0:T(8,128)(2,1)} custom-call(bf16[64,128,128]{2,1,0:T(8,128)(2,1)} %bitcast.9.kv_ref, bf16[64,128,128]{2,1,0:T(8,128)(2,1)} %bitcast.63, bf16[1040,512]{1,0:T(8,128)(2,1)} %constant.68.clone.first_ref, bf16[512,1040]{1,0:T(8,128)(2,1)} %constant.69.clone.last_ref, bf16[65,256,256]{2,1,0:T(8,128)(2,1)} %constant.70.clone.fwd_ref, ...), custom_call_target="tpu_custom_call" | custom-call | tf_op jit(solution)/shard_map/pallas_call | solution.py:105
  120.4 2.3 constant_dynamic-slice_fusion.1
  122.7 3.7 %all-to-all-start.2 = ((bf16[8,512,128]{2,1,0:T(8,128)(2,1)}), bf16[8,512,128]{2,1,0:T(8,128)(2,1)S(1)}, u32[]{:S(2)}, u32[]{:S(2)}) async-start(bf16[8,512,128]{2,1,0:T(8,128)(2,1)} %constant_dynamic-slice_fusion.1), calls=%async_computation.2 | async-start | bytes 2097152 | tf_op jit(solution)/shard_map/all_to_all | solution.py:165
  127.0 3.1 %constant_dynamic-update-slice_fusion.3 = bf16[1024,4096]{1,0:T(8,128)(2,1)} fusion(bf16[256,4096]{1,0:T(8,128)(2,1)} %collective-permute-done.1), kind=kLoop, calls=%fused_computation.35 | loop fusion | bytes 4194304
  130.2 3.1 %constant_dynamic-update-slice_fusion.2 = bf16[1024,4096]{1,0:T(8,128)(2,1)} fusion(bf16[1024,4096]{1,0:T(8,128)(2,1)} %constant_dynamic-update-slice_fusion.3, bf16[256,4096]{1,0:T(8,128)(2,1)} %collective-permute-done.2), kind=kLoop, calls=%fused_computation.34 | loop fusion | bytes 4194304
  133.3 8.3 %all-to-all-done.2 = bf16[8,512,128]{2,1,0:T(8,128)(2,1)S(1)} async-done(((bf16[8,512,128]{2,1,0:T(8,128)(2,1)}), bf16[8,512,128]{2,1,0:T(8,128)(2,1)S(1)}, u32[]{:S(2)}, u32[]{:S(2)}) %all-to-all-start.2) | async-done | bytes 1048608 | tf_op jit(solution)/shard_map/all_to_all | solution.py:165
  141.6 1.7 fusion.15
  145.2 5.7 %fusion.18 = f32[256,4096]{1,0:T(8,128)S(1)} fusion(bf16[1024,4096]{1,0:T(8,128)(2,1)} %param.17, bf16[512,1024]{1,0:T(8,128)(2,1)S(1)} %fusion.15, s32[]{:T(128)S(6)} %select_n.71), kind=kOutput, calls=%fused_computation.30 | convolution fusion | flops 2147483648 | bytes 13107204 | tf_op jit(solution)/shard_map/dot_general | solution.py:179
  150.9 3.1 %constant_dynamic-update-slice_fusion.1 = bf16[1024,4096]{1,0:T(8,128)(2,1)} fusion(bf16[1024,4096]{1,0:T(8,128)(2,1)} %constant_dynamic-update-slice_fusion.2, bf16[256,4096]{1,0:T(8,128)(2,1)} %collective-permute-done.4), kind=kLoop, calls=%fused_computation.33 | loop fusion | bytes 4194304
  154.1 3.2 %constant_dynamic-update-slice_fusion = bf16[1024,4096]{1,0:T(8,128)(2,1)} fusion(bf16[1024,4096]{1,0:T(8,128)(2,1)} %constant_dynamic-update-slice_fusion.1, bf16[256,4096]{1,0:T(8,128)(2,1)} %collective-permute-done.5), kind=kLoop, calls=%fused_computation.32 | loop fusion | bytes 4194304 | tf_op jit(solution)/shard_map/concatenate | solution.py:153
  157.3 7.4 %fusion.5 = bf16[256,4096]{1,0:T(8,128)(2,1)} fusion(f32[256,4096]{1,0:T(8,128)S(1)} %fusion.18, bf16[256,1024]{1,0:T(8,128)(2,1)S(1)} %collective-permute-done.3, bf16[1024,4096]{1,0:T(8,128)(2,1)} %constant_dynamic-update-slice_fusion), kind=kOutput, calls=%fused_computation.10 | convolution fusion | flops 2149580800 | bytes 15204352 | tf_op jit(solution)/shard_map/dot_general | solution.py:179
  165.7 3.6 %all-to-all-start.3 = ((bf16[8,512,128]{2,1,0:T(8,128)(2,1)}), bf16[8,512,128]{2,1,0:T(8,128)(2,1)S(1)}, u32[]{:S(2)}, u32[]{:S(2)}) async-start(bf16[8,512,128]{2,1,0:T(8,128)(2,1)} %constant_dynamic-slice_fusion), calls=%async_computation.3 | async-start | bytes 2097152 | tf_op jit(solution)/shard_map/all_to_all | solution.py:165
  169.3 2.7 collective-permute-start.7
  171.9 12.7 %all-to-all-done.3 = bf16[8,512,128]{2,1,0:T(8,128)(2,1)S(1)} async-done(((bf16[8,512,128]{2,1,0:T(8,128)(2,1)}), bf16[8,512,128]{2,1,0:T(8,128)(2,1)S(1)}, u32[]{:S(2)}, u32[]{:S(2)}) %all-to-all-start.3) | async-done | bytes 1048608 | tf_op jit(solution)/shard_map/all_to_all | solution.py:165
  184.6 1.7 fusion.13
  187.1 5.7 %fusion.16 = f32[256,4096]{1,0:T(8,128)S(1)} fusion(bf16[1024,4096]{1,0:T(8,128)(2,1)} %param.17, bf16[512,1024]{1,0:T(8,128)(2,1)S(1)} %fusion.13, s32[]{:T(128)S(6)} %select_n.71), kind=kOutput, calls=%fused_computation.28 | convolution fusion | flops 2147483648 | bytes 13107204 | tf_op jit(solution)/shard_map/dot_general | solution.py:179
  192.8 36.0 %collective-permute-done.6 = bf16[256,1024]{1,0:T(8,128)(2,1)S(1)} collective-permute-done((bf16[256,1024]{1,0:T(8,128)(2,1)S(1)}, bf16[256,1024]{1,0:T(8,128)(2,1)S(1)}, u32[]{:S(2)}, u32[]{:S(2)}) %collective-permute-start.6) | collective-permute-done | bytes 524320 | tf_op jit(solution)/shard_map/ppermute | solution.py:177
  228.8 5.9 %convolution_add_fusion = f32[256,4096]{1,0:T(8,128)S(1)} fusion(f32[256,4096]{1,0:T(8,128)S(1)} %fusion.16, bf16[256,1024]{1,0:T(8,128)(2,1)S(1)} %collective-permute-done.6, bf16[1024,4096]{1,0:T(8,128)(2,1)} %constant_dynamic-update-slice_fusion), kind=kOutput, calls=%fused_computation.8 | convolution fusion | flops 2148532224 | bytes 17301504 | tf_op jit(solution)/shard_map/dot_general | solution.py:179
  234.7 28.5 %collective-permute-done.7 = bf16[256,4096]{1,0:T(8,128)(2,1)} collective-permute-done((bf16[256,4096]{1,0:T(8,128)(2,1)}, bf16[256,4096]{1,0:T(8,128)(2,1)}, u32[]{:S(2)}, u32[]{:S(2)}) %collective-permute-start.7) | collective-permute-done | bytes 2097184 | tf_op jit(solution)/shard_map/ppermute | solution.py:188
  263.3 3.6 %add_convert_fusion = bf16[256,4096]{1,0:T(8,128)(2,1)} fusion(f32[256,4096]{1,0:T(8,128)S(1)} %convolution_add_fusion, bf16[256,4096]{1,0:T(8,128)(2,1)} %collective-permute-done.7), kind=kLoop, calls=%fused_computation.14 | loop fusion | flops 3145728 | bytes 8388608 | tf_op jit(solution)/shard_map/convert_element_type | solution.py:193
  (32 shorter events, 11.2 us)
Async XLA Ops:
  5.2 35.7 %all-to-all-start = ((bf16[1024,8,128]{2,0,1:T(8,128)(2,1)}), bf16[1024,8,128]{2,0,1:T(8,128)(2,1)S(1)}, u32[]{:S(2)}, u32[]{:S(2)}) async-start(bf16[1024,8,128]{2,0,1:T(8,128)(2,1)} %copy.23), calls=%async_computation | async-start | bytes 4194304 | tf_op jit(solution)/shard_map/all_to_all | solution.py:135
  15.1 51.5 %collective-permute-start.1 = (bf16[256,4096]{1,0:T(8,128)(2,1)}, bf16[256,4096]{1,0:T(8,128)(2,1)}, u32[]{:S(2)}, u32[]{:S(2)}) collective-permute-start(bf16[256,4096]{1,0:T(8,128)(2,1)} %get-tuple-element.26), channel_id=1, source_target_pairs={{0,1},{1,0},{2,3},{3,2},{4,5},{5,4},{6,7},{7,6},{8,9},{9,8},{10,11... | collective-permute-start | bytes 6291464 | tf_op jit(solution)/shard_map/ppermute | solution.py:128
  16.7 26.9 %copy-start.3 = (f32[3,2,1024]{2,1,0:T(2,128)S(1)}, f32[3,2,1024]{2,1,0:T(2,128)}, u32[]{:S(2)}) copy-start(f32[3,2,1024]{2,1,0:T(2,128)} %param.14) | copy-start | bytes 73732
  16.7 103.7 %collective-permute-start.2 = (bf16[256,4096]{1,0:T(8,128)(2,1)}, bf16[256,4096]{1,0:T(8,128)(2,1)}, u32[]{:S(2)}, u32[]{:S(2)}) collective-permute-start(bf16[256,4096]{1,0:T(8,128)(2,1)} %get-tuple-element.25), channel_id=1, source_target_pairs={{0,1},{1,0},{2,3},{3,2},{4,5},{5,4},{6,7},{7,6},{8,9},{9,8},{10,11... | collective-permute-start | bytes 6291464 | tf_op jit(solution)/shard_map/ppermute | solution.py:128
  41.0 6.9 %copy-start.2 = (bf16[1024,8,128]{2,0,1:T(8,128)(2,1)}, bf16[1024,8,128]{2,0,1:T(8,128)(2,1)S(1)}, u32[]{:S(2)}) copy-start(bf16[1024,8,128]{2,0,1:T(8,128)(2,1)S(1)} %all-to-all-done) | copy-start | bytes 6291460
  41.7 2.7 %collective-permute-start = (bf16[2,2,1024]{2,0,1:T(2,128)(2,1)S(1)}, bf16[2,2,1024]{2,0,1:T(2,128)(2,1)S(1)}, u32[]{:S(2)}, u32[]{:S(2)}) collective-permute-start(bf16[2,2,1024]{2,0,1:T(2,128)(2,1)S(1)} %slice.40), channel_id=1, source_target_pairs={{0,4},{4,8},{8,12},{12,16},{16,20},{20,24},{24,28},{1,5},{5,9},{9,... | collective-permute-start | bytes 24584 | tf_op jit(solution)/shard_map/ppermute | solution.py:19
  50.3 3.3 %copy-start = (f32[1024,2,1024]{2,0,1:T(8,128)}, f32[1024,2,1024]{2,0,1:T(8,128)S(1)}, u32[]{:S(2)}) copy-start(f32[1024,2,1024]{2,0,1:T(8,128)S(1)} %fusion.2) | copy-start | bytes 25165828
  55.9 33.3 %all-to-all-start.1 = ((bf16[1024,8,128]{2,0,1:T(8,128)(2,1)}), bf16[1024,8,128]{2,0,1:T(8,128)(2,1)}, u32[]{:S(2)}, u32[]{:S(2)}) async-start(bf16[1024,8,128]{2,0,1:T(8,128)(2,1)} %copy.24), calls=%async_computation.1 | async-start | bytes 4194304 | tf_op jit(solution)/shard_map/all_to_all | solution.py:148
  122.7 18.9 %all-to-all-start.2 = ((bf16[8,512,128]{2,1,0:T(8,128)(2,1)}), bf16[8,512,128]{2,1,0:T(8,128)(2,1)S(1)}, u32[]{:S(2)}, u32[]{:S(2)}) async-start(bf16[8,512,128]{2,1,0:T(8,128)(2,1)} %constant_dynamic-slice_fusion.1), calls=%async_computation.2 | async-start | bytes 2097152 | tf_op jit(solution)/shard_map/all_to_all | solution.py:165
  126.4 15.2 %copy-start.4 = (f32[1024]{0:T(1024)S(1)}, f32[1024]{0:T(1024)}, u32[]{:S(2)}) copy-start(f32[1024]{0:T(1024)} %param.16) | copy-start | bytes 12292
  126.5 24.5 %collective-permute-start.4 = (bf16[256,4096]{1,0:T(8,128)(2,1)}, bf16[256,4096]{1,0:T(8,128)(2,1)}, u32[]{:S(2)}, u32[]{:S(2)}) collective-permute-start(bf16[256,4096]{1,0:T(8,128)(2,1)} %collective-permute-done.1), channel_id=1, source_target_pairs={{0,4},{4,0},{8,12},{12,8},{16,20},{20,16},{24,28},{28,24},{1,5},{5... | collective-permute-start | bytes 6291464 | tf_op jit(solution)/shard_map/ppermute | solution.py:152
  126.7 27.4 %collective-permute-start.5 = (bf16[256,4096]{1,0:T(8,128)(2,1)}, bf16[256,4096]{1,0:T(8,128)(2,1)}, u32[]{:S(2)}, u32[]{:S(2)}) collective-permute-start(bf16[256,4096]{1,0:T(8,128)(2,1)} %collective-permute-done.2), channel_id=1, source_target_pairs={{0,4},{4,0},{8,12},{12,8},{16,20},{20,16},{24,28},{28,24},{1,5},{5... | collective-permute-start | bytes 6291464 | tf_op jit(solution)/shard_map/ppermute | solution.py:152
  143.6 13.7 %collective-permute-start.3 = (bf16[256,1024]{1,0:T(8,128)(2,1)S(1)}, bf16[256,1024]{1,0:T(8,128)(2,1)S(1)}, u32[]{:S(2)}, u32[]{:S(2)}) collective-permute-start(bf16[256,1024]{1,0:T(8,128)(2,1)S(1)} %maximum_select_fusion), channel_id=1, source_target_pairs={{0,1},{1,0},{2,3},{3,2},{4,5},{5,4},{6,7},{7,6},{8,9},{9,8},{10,11... | collective-permute-start | bytes 1572872 | tf_op jit(solution)/shard_map/ppermute | solution.py:177
  157.3 7.4 %copy-start.1 = (bf16[64,128,128]{2,1,0:T(8,128)(2,1)S(1)}, bf16[64,128,128]{2,1,0:T(8,128)(2,1)}, u32[]{:S(2)}) copy-start(bf16[64,128,128]{2,1,0:T(8,128)(2,1)} %shard_map.109) | copy-start | bytes 6291460
  165.7 18.9 %all-to-all-start.3 = ((bf16[8,512,128]{2,1,0:T(8,128)(2,1)}), bf16[8,512,128]{2,1,0:T(8,128)(2,1)S(1)}, u32[]{:S(2)}, u32[]{:S(2)}) async-start(bf16[8,512,128]{2,1,0:T(8,128)(2,1)} %constant_dynamic-slice_fusion), calls=%async_computation.3 | async-start | bytes 2097152 | tf_op jit(solution)/shard_map/all_to_all | solution.py:165
  169.3 94.0 %collective-permute-start.7 = (bf16[256,4096]{1,0:T(8,128)(2,1)}, bf16[256,4096]{1,0:T(8,128)(2,1)}, u32[]{:S(2)}, u32[]{:S(2)}) collective-permute-start(bf16[256,4096]{1,0:T(8,128)(2,1)} %fusion.5), channel_id=1, source_target_pairs={{0,2},{1,3},{2,0},{3,1},{4,6},{5,7},{6,4},{7,5},{8,10},{9,11},{10,... | collective-permute-start | bytes 6291464 | tf_op jit(solution)/shard_map/ppermute | solution.py:188
  186.6 42.3 %collective-permute-start.6 = (bf16[256,1024]{1,0:T(8,128)(2,1)S(1)}, bf16[256,1024]{1,0:T(8,128)(2,1)S(1)}, u32[]{:S(2)}, u32[]{:S(2)}) collective-permute-start(bf16[256,1024]{1,0:T(8,128)(2,1)S(1)} %maximum_select_fusion.1), channel_id=1, source_target_pairs={{0,1},{1,0},{2,3},{3,2},{4,5},{5,4},{6,7},{7,6},{8,9},{9,8},{10,11... | collective-permute-start | bytes 1572872 | tf_op jit(solution)/shard_map/ppermute | solution.py:177

commit v4 on v3

--- a/solution.py
+++ b/solution.py
@@ -117,6 +117,14 @@
     return out.reshape(length, channels)
 
 
+def to_channels(block):
+    shards = lax.axis_size("ctx")
+    length, channels = block.shape
+    by_owner = block.reshape(length, shards, channels // shards).transpose(1, 0, 2)
+    moved = lax.all_to_all(by_owner, "ctx", split_axis=0, concat_axis=0, tiled=True)
+    return moved.reshape(shards * length, channels // shards)
+
+
 def body(inputs, queries, kv_weight, short_taps, filter_taps, skip_gain, out_weight):
     groups, shards = lax.axis_size("tp"), lax.axis_size("ctx")
     group, core = lax.axis_index("tp"), lax.axis_index("ctx") % 2
@@ -132,7 +140,7 @@
         )
         for j in range(2)
     ]
-    taps_all = lax.all_to_all(filter_taps, "ctx", split_axis=1, concat_axis=0, tiled=True)
+    taps_all = to_channels(filter_taps)
     projected = jnp.einsum(
         "td,dkc->tkc", inputs, kv_weight, preferred_element_type=jnp.float32
     ).astype(jnp.bfloat16)
@@ -145,7 +153,8 @@
         + short_taps[2] * extended[:-2]
     )
     kv_product = (smoothed[:, 0] * smoothed[:, 1]).astype(jnp.bfloat16)
-    kv_all = lax.all_to_all(kv_product, "ctx", split_axis=1, concat_axis=0, tiled=True)
+    kv_product = lax.optimization_barrier(kv_product)
+    kv_all = to_channels(kv_product)
     kv_all, fetched[0] = lax.optimization_barrier((kv_all, fetched[0]))
     conv_all = local_conv(kv_all, taps_all)
     conv_all, fetched[1] = lax.optimization_barrier((conv_all, fetched[1]))

time: 268 us -> 266 us (level)
  waiting for transfers between devices: 109 us -> 115 us
  other arithmetic: 18.5 us -> 13.9 us
  local copies, waits for them, and re-layouts: 31.2 us -> 28.5 us
    all_to_all x2, waiting for transfers between devices: 22.6 us -> 29 us  [to_channels(): lax.all_to_all(by_owner, 'ctx', split_axis=0, concat_axis=0, tiled=True)]
    transpose x0 -> x2, local copies, waits for them, and re-layouts: none -> 4.08 us  [to_channels(): block.reshape(length, shards, channels // shards).transpose(1, 0, 2)]
    convert_element_type x1, other arithmetic: 4.18 us -> 0.72 us  [body(): kv_product = (smoothed[:, 0] * smoothed[:, 1]).astype(jnp.bfloat16)]
    unnamed x15 -> x12, local copies, waits for them, and re-layouts: 15.1 us -> 12.3 us
  transfers between devices with their start and end apart: 12 -> 12, of which waited for: 6 -> 7; matrix products, arithmetic and copies ran while one was open for 29% -> 28% of each run, Pallas kernels for 12% -> 12%
where the time goes in v4:
time: 266 us; the launch traced here: 264 us
  waiting for transfers between devices  115 us (43%)
  matrix products  48.6 us (18%)
  Pallas kernels  31.2 us (12%)
  local copies, waits for them, and re-layouts  28.5 us (11%)
  starting transfers between devices  26.8 us (10%)
  other arithmetic  13.9 us (5%)
    ppermute x2, waiting for transfers between devices, pair_sum(): received = lax.ppermute(sent, 'tp', mates)  35.1 us
    pallas_call x1, Pallas kernels, local_conv(): pl.pallas_call(functools.partial(conv_kernel, half, per_step, 0.5 / lengt...  31.2 us
    all_to_all x2, waiting for transfers between devices, to_channels(): lax.all_to_all(by_owner, 'ctx', split_axis=0, concat_axis=0, tiled=True)  29 us
    ppermute x1, waiting for transfers between devices, body(): arrived.append(lax.ppermute(part, 'tp', ring))  28.7 us
    dot_general x1, matrix products, body(): jnp.einsum('td,dkc->tkc', inputs, kv_weight, preferred_element_type=jnp.f...  23.9 us
    all_to_all x2, waiting for transfers between devices, pair_sum(): lax.all_to_all(conv_part, 'ctx', split_axis=0, concat_axis=1, tiled=True)  21.6 us
    dot_general x2, matrix products, pair_sum(): jnp.dot(received, mate_weight, preferred_element_type=jnp.float32)  13.3 us
    unnamed x12, local copies, waits for them, and re-layouts  12.3 us
  transfers between devices with their start and end apart: 12, of which 7 were waited for; matrix products, arithmetic and copies ran while one was open for 28% of the time, Pallas kernels for 12%

profile of v4, /device:TPU:0, one launch (start us, length us, event | category | flops | bytes accessed | tf_op | source)
XLA Modules:
  0.0 264.4 jit_solution(11779728053821802354)
XLA Ops:
  0.0 4.7 %constant_dynamic-slice_fusion.2 = (bf16[256,4096]{1,0:T(8,128)(2,1)}, bf16[256,4096]{1,0:T(8,128)(2,1)}) fusion(bf16[1024,4096]{1,0:T(8,128)(2,1)} %param.17, s32[]{:T(128)S(6)} %select_n.70, s32[]{:T(128)S(6)} %select_n.69), kind=kLoop, calls=%fused_computation.43 | loop fusion | bytes 8388616 | tf_op jit(solution)/shard_map/dynamic_slice | solution.py:137
  4.7 3.0 %collective-permute-start.1 = (bf16[256,4096]{1,0:T(8,128)(2,1)}, bf16[256,4096]{1,0:T(8,128)(2,1)}, u32[]{:S(2)}, u32[]{:S(2)}) collective-permute-start(bf16[256,4096]{1,0:T(8,128)(2,1)} %get-tuple-element.26), channel_id=1, source_target_pairs={{0,1},{1,0},{2,3},{3,2},{4,5},{5,4},{6,7},{7,6},{8,9},{9,8},{10,11... | collective-permute-start | bytes 6291464 | tf_op jit(solution)/shard_map/ppermute | solution.py:136
  7.7 2.9 %copy.22 = bf16[1024,1024]{0,1:T(8,128)(2,1)S(1)} copy(bf16[1024,1024]{1,0:T(8,128)(2,1)} %param.15) | data formatting | bytes 4194304 | tf_op args[4]
  10.6 2.4 copy.23
  13.0 3.7 %all-to-all-start = ((bf16[8,1024,128]{2,1,0:T(8,128)(2,1)}), bf16[8,1024,128]{2,1,0:T(8,128)(2,1)S(1)}, u32[]{:S(2)}, u32[]{:S(2)}) async-start(bf16[8,1024,128]{2,1,0:T(8,128)(2,1)} %copy.23), calls=%async_computation | async-start | bytes 4194304 | tf_op jit(solution)/shard_map/all_to_all | solution.py:124
  17.2 23.9 %fusion.7 = bf16[1024,2,1024]{2,0,1:T(8,128)(2,1)} fusion(bf16[4096,2,1024]{2,1,0:T(2,128)(2,1)} %param.13, bf16[1024,4096]{1,0:T(8,128)(2,1)} %param.11), kind=kOutput, calls=%fused_computation.15 | convolution fusion | flops 17181966336 | bytes 29360128 | tf_op jit(solution)/shard_map/td,dkc->tkc/dot_general | solution.py:144
  41.1 2.3 all-to-all-done
  46.2 3.4 %maximum_convert_fusion = f32[1026,2,1024]{2,0,1:T(8,128)S(1)} fusion(bf16[1024,2,1024]{2,0,1:T(8,128)(2,1)} %fusion.7, bf16[2,2,1024]{2,0,1:T(2,128)(2,1)S(1)} %collective-permute-done), kind=kLoop, calls=%fused_computation.11 | loop fusion | flops 8404992 | bytes 12607488 | tf_op jit(solution)/shard_map/convert_element_type | solution.py:149
  49.7 2.5 fusion.2
  52.9 1.7 bitcast_bitcast_fusion
  54.6 5.6 %all-to-all-start.1 = ((bf16[8,1024,128]{2,1,0:T(8,128)(2,1)}), bf16[8,1024,128]{2,1,0:T(8,128)(2,1)}, u32[]{:S(2)}, u32[]{:S(2)}) async-start(bf16[8,1024,128]{2,1,0:T(8,128)(2,1)} %bitcast_bitcast_fusion), calls=%async_computation.1 | async-start | bytes 4194304 | tf_op jit(solution)/shard_map/all_to_all | solution.py:124
  60.2 26.7 %all-to-all-done.1 = bf16[8,1024,128]{2,1,0:T(8,128)(2,1)} async-done(((bf16[8,1024,128]{2,1,0:T(8,128)(2,1)}), bf16[8,1024,128]{2,1,0:T(8,128)(2,1)}, u32[]{:S(2)}, u32[]{:S(2)}) %all-to-all-start.1) | async-done | bytes 2097184 | tf_op jit(solution)/shard_map/all_to_all | solution.py:124
  86.9 31.2 %shard_map.109 = bf16[64,128,128]{2,1,0:T(8,128)(2,1)} custom-call(bf16[64,128,128]{2,1,0:T(8,128)(2,1)} %bitcast.10.kv_ref, bf16[64,128,128]{2,1,0:T(8,128)(2,1)} %bitcast.58, bf16[1040,512]{1,0:T(8,128)(2,1)} %constant.66.clone.first_ref, bf16[512,1040]{1,0:T(8,128)(2,1)} %constant.67.clone.last_ref, bf16[65,256,256]{2,1,0:T(8,128)(2,1)} %constant.68.clone.fwd_ref, ...), custom_call_target="tpu_custom_call" | custom-call | tf_op jit(solution)/shard_map/pallas_call | solution.py:105
  118.6 2.3 constant_dynamic-slice_fusion.1
  120.9 3.7 %all-to-all-start.2 = ((bf16[8,512,128]{2,1,0:T(8,128)(2,1)}), bf16[8,512,128]{2,1,0:T(8,128)(2,1)S(1)}, u32[]{:S(2)}, u32[]{:S(2)}) async-start(bf16[8,512,128]{2,1,0:T(8,128)(2,1)} %constant_dynamic-slice_fusion.1), calls=%async_computation.2 | async-start | bytes 2097152 | tf_op jit(solution)/shard_map/all_to_all | solution.py:174
  124.7 3.1 %constant_dynamic-update-slice_fusion.3 = bf16[1024,4096]{1,0:T(8,128)(2,1)} fusion(bf16[256,4096]{1,0:T(8,128)(2,1)} %collective-permute-done.1), kind=kLoop, calls=%fused_computation.35 | loop fusion | bytes 4194304
  127.8 3.1 %constant_dynamic-update-slice_fusion.2 = bf16[1024,4096]{1,0:T(8,128)(2,1)} fusion(bf16[1024,4096]{1,0:T(8,128)(2,1)} %constant_dynamic-update-slice_fusion.3, bf16[256,4096]{1,0:T(8,128)(2,1)} %collective-permute-done.2), kind=kLoop, calls=%fused_computation.34 | loop fusion | bytes 4194304
  130.9 8.9 %all-to-all-done.2 = bf16[8,512,128]{2,1,0:T(8,128)(2,1)S(1)} async-done(((bf16[8,512,128]{2,1,0:T(8,128)(2,1)}), bf16[8,512,128]{2,1,0:T(8,128)(2,1)S(1)}, u32[]{:S(2)}, u32[]{:S(2)}) %all-to-all-start.2) | async-done | bytes 1048608 | tf_op jit(solution)/shard_map/all_to_all | solution.py:174
  139.9 1.7 fusion.16
  142.6 5.7 %fusion.19 = f32[256,4096]{1,0:T(8,128)S(1)} fusion(bf16[1024,4096]{1,0:T(8,128)(2,1)} %param.17, bf16[512,1024]{1,0:T(8,128)(2,1)S(1)} %fusion.16, s32[]{:T(128)S(6)} %select_n.71), kind=kOutput, calls=%fused_computation.30 | convolution fusion | flops 2147483648 | bytes 13107204 | tf_op jit(solution)/shard_map/dot_general | solution.py:188
  148.3 3.2 %constant_dynamic-update-slice_fusion.1 = bf16[1024,4096]{1,0:T(8,128)(2,1)} fusion(bf16[1024,4096]{1,0:T(8,128)(2,1)} %constant_dynamic-update-slice_fusion.2, bf16[256,4096]{1,0:T(8,128)(2,1)} %collective-permute-done.4), kind=kLoop, calls=%fused_computation.33 | loop fusion | bytes 4194304
  151.5 3.2 %constant_dynamic-update-slice_fusion = bf16[1024,4096]{1,0:T(8,128)(2,1)} fusion(bf16[1024,4096]{1,0:T(8,128)(2,1)} %constant_dynamic-update-slice_fusion.1, bf16[256,4096]{1,0:T(8,128)(2,1)} %collective-permute-done.5), kind=kLoop, calls=%fused_computation.32 | loop fusion | bytes 4194304 | tf_op jit(solution)/shard_map/concatenate | solution.py:162
  154.7 7.4 %fusion.5 = bf16[256,4096]{1,0:T(8,128)(2,1)} fusion(f32[256,4096]{1,0:T(8,128)S(1)} %fusion.19, bf16[256,1024]{1,0:T(8,128)(2,1)S(1)} %collective-permute-done.3, bf16[1024,4096]{1,0:T(8,128)(2,1)} %constant_dynamic-update-slice_fusion), kind=kOutput, calls=%fused_computation.10 | convolution fusion | flops 2149580800 | bytes 15204352 | tf_op jit(solution)/shard_map/dot_general | solution.py:188
  163.1 3.6 %all-to-all-start.3 = ((bf16[8,512,128]{2,1,0:T(8,128)(2,1)}), bf16[8,512,128]{2,1,0:T(8,128)(2,1)S(1)}, u32[]{:S(2)}, u32[]{:S(2)}) async-start(bf16[8,512,128]{2,1,0:T(8,128)(2,1)} %constant_dynamic-slice_fusion), calls=%async_computation.3 | async-start | bytes 2097152 | tf_op jit(solution)/shard_map/all_to_all | solution.py:174
  166.7 2.6 %collective-permute-start.7 = (bf16[256,4096]{1,0:T(8,128)(2,1)}, bf16[256,4096]{1,0:T(8,128)(2,1)}, u32[]{:S(2)}, u32[]{:S(2)}) collective-permute-start(bf16[256,4096]{1,0:T(8,128)(2,1)} %fusion.5), channel_id=1, source_target_pairs={{0,2},{1,3},{2,0},{3,1},{4,6},{5,7},{6,4},{7,5},{8,10},{9,11},{10,... | collective-permute-start | bytes 6291464 | tf_op jit(solution)/shard_map/ppermute | solution.py:197
  169.4 12.7 %all-to-all-done.3 = bf16[8,512,128]{2,1,0:T(8,128)(2,1)S(1)} async-done(((bf16[8,512,128]{2,1,0:T(8,128)(2,1)}), bf16[8,512,128]{2,1,0:T(8,128)(2,1)S(1)}, u32[]{:S(2)}, u32[]{:S(2)}) %all-to-all-start.3) | async-done | bytes 1048608 | tf_op jit(solution)/shard_map/all_to_all | solution.py:174
  182.0 1.7 fusion.14
  185.4 5.7 %fusion.17 = f32[256,4096]{1,0:T(8,128)S(1)} fusion(bf16[1024,4096]{1,0:T(8,128)(2,1)} %param.17, bf16[512,1024]{1,0:T(8,128)(2,1)S(1)} %fusion.14, s32[]{:T(128)S(6)} %select_n.71), kind=kOutput, calls=%fused_computation.28 | convolution fusion | flops 2147483648 | bytes 13107204 | tf_op jit(solution)/shard_map/dot_general | solution.py:188
  191.1 35.1 %collective-permute-done.6 = bf16[256,1024]{1,0:T(8,128)(2,1)S(1)} collective-permute-done((bf16[256,1024]{1,0:T(8,128)(2,1)S(1)}, bf16[256,1024]{1,0:T(8,128)(2,1)S(1)}, u32[]{:S(2)}, u32[]{:S(2)}) %collective-permute-start.6) | collective-permute-done | bytes 524320 | tf_op jit(solution)/shard_map/ppermute | solution.py:186
  226.2 5.9 %convolution_add_fusion = f32[256,4096]{1,0:T(8,128)S(1)} fusion(f32[256,4096]{1,0:T(8,128)S(1)} %fusion.17, bf16[256,1024]{1,0:T(8,128)(2,1)S(1)} %collective-permute-done.6, bf16[1024,4096]{1,0:T(8,128)(2,1)} %constant_dynamic-update-slice_fusion), kind=kOutput, calls=%fused_computation.8 | convolution fusion | flops 2148532224 | bytes 17301504 | tf_op jit(solution)/shard_map/dot_general | solution.py:188
  232.1 28.7 %collective-permute-done.7 = bf16[256,4096]{1,0:T(8,128)(2,1)} collective-permute-done((bf16[256,4096]{1,0:T(8,128)(2,1)}, bf16[256,4096]{1,0:T(8,128)(2,1)}, u32[]{:S(2)}, u32[]{:S(2)}) %collective-permute-start.7) | collective-permute-done | bytes 2097184 | tf_op jit(solution)/shard_map/ppermute | solution.py:197
  260.8 3.6 %add_convert_fusion = bf16[256,4096]{1,0:T(8,128)(2,1)} fusion(f32[256,4096]{1,0:T(8,128)S(1)} %convolution_add_fusion, bf16[256,4096]{1,0:T(8,128)(2,1)} %collective-permute-done.7), kind=kLoop, calls=%fused_computation.14 | loop fusion | flops 3145728 | bytes 8388608 | tf_op jit(solution)/shard_map/convert_element_type | solution.py:202
  (28 shorter events, 8.3 us)
Async XLA Ops:
  4.7 55.5 %collective-permute-start.1 = (bf16[256,4096]{1,0:T(8,128)(2,1)}, bf16[256,4096]{1,0:T(8,128)(2,1)}, u32[]{:S(2)}, u32[]{:S(2)}) collective-permute-start(bf16[256,4096]{1,0:T(8,128)(2,1)} %get-tuple-element.26), channel_id=1, source_target_pairs={{0,1},{1,0},{2,3},{3,2},{4,5},{5,4},{6,7},{7,6},{8,9},{9,8},{10,11... | collective-permute-start | bytes 6291464 | tf_op jit(solution)/shard_map/ppermute | solution.py:136
  13.0 30.4 %all-to-all-start = ((bf16[8,1024,128]{2,1,0:T(8,128)(2,1)}), bf16[8,1024,128]{2,1,0:T(8,128)(2,1)S(1)}, u32[]{:S(2)}, u32[]{:S(2)}) async-start(bf16[8,1024,128]{2,1,0:T(8,128)(2,1)} %copy.23), calls=%async_computation | async-start | bytes 4194304 | tf_op jit(solution)/shard_map/all_to_all | solution.py:124
  16.7 28.7 %copy-start.2 = (f32[3,2,1024]{2,1,0:T(2,128)S(1)}, f32[3,2,1024]{2,1,0:T(2,128)}, u32[]{:S(2)}) copy-start(f32[3,2,1024]{2,1,0:T(2,128)} %param.14) | copy-start | bytes 73732
  16.7 101.4 %collective-permute-start.2 = (bf16[256,4096]{1,0:T(8,128)(2,1)}, bf16[256,4096]{1,0:T(8,128)(2,1)}, u32[]{:S(2)}, u32[]{:S(2)}) collective-permute-start(bf16[256,4096]{1,0:T(8,128)(2,1)} %get-tuple-element.25), channel_id=1, source_target_pairs={{0,1},{1,0},{2,3},{3,2},{4,5},{5,4},{6,7},{7,6},{8,9},{9,8},{10,11... | collective-permute-start | bytes 6291464 | tf_op jit(solution)/shard_map/ppermute | solution.py:136
  43.4 6.3 %copy-start.1 = (bf16[8,1024,128]{2,1,0:T(8,128)(2,1)}, bf16[8,1024,128]{2,1,0:T(8,128)(2,1)S(1)}, u32[]{:S(2)}) copy-start(bf16[8,1024,128]{2,1,0:T(8,128)(2,1)S(1)} %all-to-all-done) | copy-start | bytes 6291460
  44.1 2.1 collective-permute-start
  54.6 32.3 %all-to-all-start.1 = ((bf16[8,1024,128]{2,1,0:T(8,128)(2,1)}), bf16[8,1024,128]{2,1,0:T(8,128)(2,1)}, u32[]{:S(2)}, u32[]{:S(2)}) async-start(bf16[8,1024,128]{2,1,0:T(8,128)(2,1)} %bitcast_bitcast_fusion), calls=%async_computation.1 | async-start | bytes 4194304 | tf_op jit(solution)/shard_map/all_to_all | solution.py:124
  118.1 30.2 %collective-permute-start.4 = (bf16[256,4096]{1,0:T(8,128)(2,1)}, bf16[256,4096]{1,0:T(8,128)(2,1)}, u32[]{:S(2)}, u32[]{:S(2)}) collective-permute-start(bf16[256,4096]{1,0:T(8,128)(2,1)} %collective-permute-done.1), channel_id=1, source_target_pairs={{0,4},{4,0},{8,12},{12,8},{16,20},{20,16},{24,28},{28,24},{1,5},{5... | collective-permute-start | bytes 6291464 | tf_op jit(solution)/shard_map/ppermute | solution.py:161
  118.1 33.3 %collective-permute-start.5 = (bf16[256,4096]{1,0:T(8,128)(2,1)}, bf16[256,4096]{1,0:T(8,128)(2,1)}, u32[]{:S(2)}, u32[]{:S(2)}) collective-permute-start(bf16[256,4096]{1,0:T(8,128)(2,1)} %collective-permute-done.2), channel_id=1, source_target_pairs={{0,4},{4,0},{8,12},{12,8},{16,20},{20,16},{24,28},{28,24},{1,5},{5... | collective-permute-start | bytes 6291464 | tf_op jit(solution)/shard_map/ppermute | solution.py:161
  120.9 18.9 %all-to-all-start.2 = ((bf16[8,512,128]{2,1,0:T(8,128)(2,1)}), bf16[8,512,128]{2,1,0:T(8,128)(2,1)S(1)}, u32[]{:S(2)}, u32[]{:S(2)}) async-start(bf16[8,512,128]{2,1,0:T(8,128)(2,1)} %constant_dynamic-slice_fusion.1), calls=%async_computation.2 | async-start | bytes 2097152 | tf_op jit(solution)/shard_map/all_to_all | solution.py:174
  124.7 15.2 %copy-start.3 = (f32[1024]{0:T(1024)S(1)}, f32[1024]{0:T(1024)}, u32[]{:S(2)}) copy-start(f32[1024]{0:T(1024)} %param.16) | copy-start | bytes 12292
  141.8 12.9 %collective-permute-start.3 = (bf16[256,1024]{1,0:T(8,128)(2,1)S(1)}, bf16[256,1024]{1,0:T(8,128)(2,1)S(1)}, u32[]{:S(2)}, u32[]{:S(2)}) collective-permute-start(bf16[256,1024]{1,0:T(8,128)(2,1)S(1)} %maximum_select_fusion), channel_id=1, source_target_pairs={{0,1},{1,0},{2,3},{3,2},{4,5},{5,4},{6,7},{7,6},{8,9},{9,8},{10,11... | collective-permute-start | bytes 1572872 | tf_op jit(solution)/shard_map/ppermute | solution.py:186
  154.7 7.4 %copy-start = (bf16[64,128,128]{2,1,0:T(8,128)(2,1)S(1)}, bf16[64,128,128]{2,1,0:T(8,128)(2,1)}, u32[]{:S(2)}) copy-start(bf16[64,128,128]{2,1,0:T(8,128)(2,1)} %shard_map.109) | copy-start | bytes 6291460
  163.1 18.9 %all-to-all-start.3 = ((bf16[8,512,128]{2,1,0:T(8,128)(2,1)}), bf16[8,512,128]{2,1,0:T(8,128)(2,1)S(1)}, u32[]{:S(2)}, u32[]{:S(2)}) async-start(bf16[8,512,128]{2,1,0:T(8,128)(2,1)} %constant_dynamic-slice_fusion), calls=%async_computation.3 | async-start | bytes 2097152 | tf_op jit(solution)/shard_map/all_to_all | solution.py:174
  166.7 94.1 %collective-permute-start.7 = (bf16[256,4096]{1,0:T(8,128)(2,1)}, bf16[256,4096]{1,0:T(8,128)(2,1)}, u32[]{:S(2)}, u32[]{:S(2)}) collective-permute-start(bf16[256,4096]{1,0:T(8,128)(2,1)} %fusion.5), channel_id=1, source_target_pairs={{0,2},{1,3},{2,0},{3,1},{4,6},{5,7},{6,4},{7,5},{8,10},{9,11},{10,... | collective-permute-start | bytes 6291464 | tf_op jit(solution)/shard_map/ppermute | solution.py:197
  184.0 42.2 %collective-permute-start.6 = (bf16[256,1024]{1,0:T(8,128)(2,1)S(1)}, bf16[256,1024]{1,0:T(8,128)(2,1)S(1)}, u32[]{:S(2)}, u32[]{:S(2)}) collective-permute-start(bf16[256,1024]{1,0:T(8,128)(2,1)S(1)} %maximum_select_fusion.1), channel_id=1, source_target_pairs={{0,1},{1,0},{2,3},{3,2},{4,5},{5,4},{6,7},{7,6},{8,9},{9,8},{10,11... | collective-permute-start | bytes 1572872 | tf_op jit(solution)/shard_map/ppermute | solution.py:186
